TPU v7x, 128 devices: a whole 4x4x4 slice. The times are simulated.
128 devices in a mesh: fsdp: 32 (over y_hi, z, x), tp: 4 (over y_lo, core).
Axes of the slice: x: 4, y: 4 (y_hi: 2, y_lo: 2; y = y_hi * 2 + y_lo), z: 4, core: 2. Of those that a mesh axis runs over, the one named last changes fastest.
Arguments:
- tokens: bfloat16 [16384, 1024], P(('fsdp', 'tp')), may hold values from -6 to 6
- segments: int32 [16384], P('fsdp'), may hold values from 0 to 1, as said below
- mix_gain: bfloat16 [1024], replicated, may hold values from 0.5 to 1.5
- in_weight: bfloat16 [3, 1024, 1024], P(None, 'fsdp', 'tp'), may hold values from -0.1875 to 0.1875
- conv_weight: bfloat16 [3, 1024], replicated, may hold values from -3.5 to 3.5
- out_weight: bfloat16 [1024, 1024], P('tp', 'fsdp'), may hold values from -0.1875 to 0.1875
- ffn_gain: bfloat16 [1024], replicated, may hold values from 0.5 to 1.5
- up_gate_weight: bfloat16 [2, 1024, 4608], P(None, 'fsdp', 'tp'), may hold values from -0.1875 to 0.1875
- down_weight: bfloat16 [4608, 1024], P('tp', 'fsdp'), may hold values from -0.09375 to 0.09375
- cotangent: bfloat16 [16384, 1024], P(('fsdp', 'tp')), may hold values from -24 to 24
Outputs:
- mixed: bfloat16 [16384, 1024], P(('fsdp', 'tp'))
- input_grad: float32 [16384, 1024], P(('fsdp', 'tp'))
- mix_gain_grad: float32 [1024], replicated
- in_weight_grad: float32 [3, 1024, 1024], P(None, 'fsdp', 'tp')
- conv_weight_grad: float32 [3, 1024], replicated
- out_weight_grad: float32 [1024, 1024], P('tp', 'fsdp')
- ffn_gain_grad: float32 [1024], replicated
- up_gate_grad: float32 [2, 1024, 4608], P(None, 'fsdp', 'tp')
- down_grad: float32 [4608, 1024], P('tp', 'fsdp')
Inputs may be any that keep to these rules, and one draw needn't show every extreme that they name: `segments`: tokens form documents in order; each token holds its document's number modulo 2, so the value changes exactly where a document starts. Every document but the last has 200 to 2000 tokens, the last has 2 or more.
All inputs are finite; a program needn't handle non-finite values.
Results may differ from a plain program's by a relative error of at most 0.024.
Values may be sent and summed in bfloat16 or wider, within the bound.
No kernel may reach another device: no remote copies, remote signals or barrier semaphores. Data moves between devices by JAX's collectives and lax.ppermute only.
A program may use at most 128 MiB of HBM per device.

v0:
```python
import jax
import jax.numpy as jnp
from jax import lax
from jax.sharding import Mesh, PartitionSpec as P

EPSILON = 1e-05
F32 = jnp.float32
BF16 = jnp.bfloat16
FSDP = ("yh", "z", "x")
TP = ("yl", "core")
ALL = FSDP + TP


def dot(lhs, rhs, lhs_dim, rhs_dim):
    return lax.dot_general(
        lhs, rhs, (((lhs_dim,), (rhs_dim,)), ((), ())), preferred_element_type=F32
    )


def shifted(value, axis, by):
    size = lax.axis_size(axis)
    return lax.ppermute(value, axis, [(i, (i + by) % size) for i in range(size)])


def swapped(value, axis):
    return lax.ppermute(value, axis, [(0, 1), (1, 0)])


def norm_parts(values):
    scale = lax.rsqrt(jnp.mean(values * values, axis=-1, keepdims=True) + EPSILON)
    return (scale, values * scale)


def norm_back(grad_out, gain, scale, normed):
    grad_norm = grad_out * gain
    return scale * (grad_norm - normed * jnp.mean(grad_norm * normed, axis=-1, keepdims=True))


def after(value, *earlier):
    return lax.optimization_barrier((value,) + earlier)[0]


def no_sooner(value, earlier):
    corner = lax.slice(earlier, (0,) * earlier.ndim, (1,) * earlier.ndim).reshape(())
    return value + jnp.minimum(jnp.abs(corner), 0).astype(value.dtype)


def put(block, whole, dim, index):
    return lax.dynamic_update_slice_in_dim(whole, jnp.expand_dims(block, dim), index, dim)


def take(whole, dim, index):
    return lax.dynamic_index_in_dim(whole, index, dim, keepdims=False)


def ring_gather(block, axis, dim):
    me = lax.axis_index(axis)
    whole = jnp.zeros(block.shape[:dim] + (4,) + block.shape[dim:], block.dtype)
    whole = put(block, whole, dim, me)
    for by in (1, 3, 2):
        whole = put(shifted(block, axis, by), whole, dim, (me - by) % 4)
    return whole


def ring_gather_passing(block, axis, dim):
    me = lax.axis_index(axis)
    before = shifted(block, axis, 1)
    behind = shifted(block, axis, -1)
    far = jnp.concatenate([shifted(before[:1], axis, 1), shifted(behind[1:], axis, -1)])
    whole = jnp.zeros(block.shape[:dim] + (4,) + block.shape[dim:], block.dtype)
    for value, by in ((block, 0), (before, 3), (behind, 1), (far, 2)):
        whole = put(value, whole, dim, (me + by) % 4)
    return whole


def pair_rows(shard):
    other = swapped(shard, "yh")
    first = lax.axis_index("yh") == 0
    return jnp.stack([jnp.where(first, shard, other), jnp.where(first, other, shard)])


def gather_rows(first, second):
    pair = pair_rows(jnp.concatenate([first, second], axis=1))
    columns = first.shape[1]
    one = ring_gather(ring_gather(pair[:, :, :columns], "z", 1), "x", 2)
    two = ring_gather_passing(ring_gather(pair[:, :, columns:], "x", 1), "z", 1)
    return one.reshape(-1, columns), two.reshape(-1, second.shape[1])


def ring_scatter(whole, axis, dim, earlier):
    me = lax.axis_index(axis)
    total = take(whole, dim, me).astype(F32)
    for by in (1, 3, 2):
        part = no_sooner(take(whole, dim, (me + by) % 4), earlier)
        total = total + shifted(part, axis, by).astype(F32)
    return total


def exchange_sum(whole, axes):
    count = 1
    for axis in axes:
        count *= lax.axis_size(axis)
    parts = lax.all_to_all(whole.reshape(count, -1, whole.shape[1]), axes, 0, 0)
    return jnp.sum(parts.astype(F32), axis=0)


def x_outermost(rows):
    parts = rows.reshape(rows.shape[0], 2, 4, 4, -1).transpose(0, 3, 2, 1, 4)
    return parts.reshape(rows.shape)


def z_outermost(rows):
    parts = rows.reshape(rows.shape[0], 2, 4, 4, -1).swapaxes(1, 2)
    return parts.reshape(rows.shape)


def gather_tokens(block):
    return gather_core(block, swapped(block, "yl"))


def gather_core(block, far):
    pair = jnp.concatenate([block, far])
    return jnp.concatenate([pair, swapped(pair, "core")])


def scatter_tokens(terms, earlier=None):
    half = terms.shape[0] // 2
    pair = terms[:half].astype(F32) + swapped(terms[half:].astype(BF16), "core").astype(F32)
    rows = half // 2
    far = swapped(pair[rows:].astype(BF16), "yl")
    if earlier is not None:
        far = no_sooner(far, earlier)
    return pair[:rows] + far.astype(F32)


def reordered(rows):
    blocks = rows.reshape(4, -1, rows.shape[1])
    me = lax.axis_index("core") * 2 + lax.axis_index("yl")
    return jnp.concatenate([take(blocks, 0, me ^ other) for other in (0, 2, 1, 3)])


def restored(rows):
    blocks = rows.reshape(4, -1, rows.shape[1])
    me = lax.axis_index("yl") * 2 + lax.axis_index("core")
    return jnp.concatenate([take(blocks, 0, me ^ other) for other in (0, 2, 1, 3)])


def along_tokens(value, by):
    pairs = [(i, i + by) for i in range(32) if 0 <= i + by < 32]
    return lax.ppermute(value, FSDP, pairs)


def local(
    tokens,
    segments,
    mix_gain,
    in_weight,
    conv_weight,
    out_weight,
    ffn_gain,
    up_gate_weight,
    down_weight,
    cotangent,
):
    width = tokens.shape[1]
    chan_dev = in_weight.shape[2]
    hidden_dev = up_gate_weight.shape[2]
    shard_rows = in_weight.shape[1]
    tp_index = lax.axis_index("yl") * 2 + lax.axis_index("core")

    in_shard = jnp.concatenate([in_weight[0], in_weight[1], in_weight[2]], axis=1)
    in_full, second_full = gather_rows(
        in_shard, jnp.concatenate([out_weight.T, down_weight.T], axis=1)
    )
    out_full = second_full[:, :chan_dev]
    down_full = second_full[:, chan_dev:]
    up_gate_full = lax.all_gather(up_gate_weight, FSDP, axis=1, tiled=True)

    conv_local = lax.dynamic_slice_in_dim(conv_weight, tp_index * chan_dev, chan_dev, 1).astype(F32)
    tok_f32 = tokens.astype(F32)
    scale_one, normed_one = norm_parts(tok_f32)
    gain_one = mix_gain.astype(F32)
    mix_rows = reordered(gather_tokens((normed_one * gain_one).astype(BF16)))
    group_rows = mix_rows.shape[0]
    projected = dot(mix_rows, in_full, 1, 0).astype(BF16)
    proj_b = projected[:, :chan_dev].astype(F32)
    proj_c = projected[:, chan_dev : 2 * chan_dev].astype(F32)
    proj_x = projected[:, 2 * chan_dev :].astype(F32)
    product = proj_b * proj_x
    parity = (segments % 2).astype(F32)
    parity_row = jnp.zeros((1, chan_dev), F32).at[0, :2].set(parity[-2:])
    rim_send = jnp.concatenate([product[-2:], parity_row], axis=0)
    rim_recv = along_tokens(rim_send, 1)
    padded = jnp.concatenate([rim_recv[:2], product], axis=0)
    parity_pad = jnp.concatenate([rim_recv[2, :2], parity])
    masks = [
        (parity_pad[2 - offset : 2 - offset + group_rows] == parity).astype(F32)[:, None]
        for offset in range(3)
    ]
    conv_out = jnp.zeros_like(product)
    for offset in range(3):
        conv_out = (
            conv_out
            + conv_local[2 - offset] * masks[offset] * padded[2 - offset : 2 - offset + group_rows]
        )
    mixer_in = (proj_c * conv_out).astype(BF16)
    mixer_out = scatter_tokens(dot(restored(mixer_in), out_full, 1, 1))
    middle = tok_f32 + mixer_out
    scale_two, normed_two = norm_parts(middle)
    gain_two = ffn_gain.astype(F32)
    cot_rows = gather_tokens(after(cotangent, mix_rows))
    second = (normed_two * gain_two).astype(BF16)
    ffn_rows = gather_core(second, after(swapped(second, "yl"), up_gate_full))
    grad_hidden = dot(cot_rows, down_full, 1, 0)
    gate_val = dot(ffn_rows, up_gate_full[0], 1, 0)
    up_val = dot(ffn_rows, up_gate_full[1], 1, 0)
    sigma = jax.nn.sigmoid(gate_val)
    hidden = (gate_val * sigma * up_val).astype(BF16)
    grad_up = grad_hidden * gate_val * sigma
    grad_gate = grad_hidden * up_val * sigma * (1.0 + gate_val * (1.0 - sigma))
    grad_gate = grad_gate.astype(BF16)
    grad_up = grad_up.astype(BF16)
    grad_down = dot(z_outermost(cot_rows), hidden, 0, 0).astype(BF16)
    down_part = exchange_sum(grad_down, ("z",)).astype(BF16)
    grad_gate = after(grad_gate, grad_down)
    grad_rows_two = dot(grad_gate, up_gate_full[0], 1, 1) + dot(grad_up, up_gate_full[1], 1, 1)
    grad_gate_w = dot(
        x_outermost(after(ffn_rows, grad_rows_two)), jnp.concatenate([grad_gate, grad_up], axis=1), 0, 0
    ).astype(BF16)
    gate_part = lax.psum_scatter(grad_gate_w, "x", scatter_dimension=0, tiled=True)
    gate_part = lax.psum_scatter(gate_part, "z", scatter_dimension=0, tiled=True)
    grad_normed_two = scatter_tokens(grad_rows_two)
    gain_two_grad = jnp.sum(grad_normed_two * normed_two, axis=0)
    grad_middle = cotangent.astype(F32) + norm_back(grad_normed_two, gain_two, scale_two, normed_two)
    grad_mid_low = grad_middle.astype(BF16)
    grad_mid_far = no_sooner(swapped(grad_mid_low, "yl"), down_part)
    grad_mix_rows = reordered(gather_core(grad_mid_low, grad_mid_far))
    ffn_terms = dot(after(hidden, grad_mid_low), down_full, 1, 1)
    mixed = (middle + scatter_tokens(after(ffn_terms, grad_mix_rows))).astype(BF16)
    grad_mixer_in = dot(grad_mix_rows, out_full, 1, 0)
    grad_out_w = dot(grad_mix_rows, mixer_in, 0, 0).astype(BF16)
    grad_c = grad_mixer_in * conv_out
    grad_conv = grad_mixer_in * proj_c
    grad_padded = jnp.zeros((group_rows + 2, chan_dev), F32)
    conv_grads = []
    for offset in range(3):
        masked = masks[offset] * grad_conv
        grad_padded = grad_padded + jnp.pad(
            conv_local[2 - offset] * masked, ((2 - offset, offset), (0, 0))
        )
        conv_grads.append(jnp.sum(masked * padded[2 - offset : 2 - offset + group_rows], axis=0))
    conv_grad_local = jnp.stack([conv_grads[2], conv_grads[1], conv_grads[0]])
    rim_back = along_tokens(grad_padded[:2], -1)
    grad_product = grad_padded[2:] + jnp.pad(rim_back, ((group_rows - 2, 0), (0, 0)))
    grad_proj = jnp.concatenate(
        [
            (grad_product * proj_x).astype(BF16),
            grad_c.astype(BF16),
            (grad_product * proj_b).astype(BF16),
        ],
        axis=1,
    )
    grad_in_w = dot(mix_rows, grad_proj, 0, 0).astype(BF16)
    grad_rows_one = dot(grad_proj, in_full, 1, 1)
    gain_one_grad = jnp.sum(grad_rows_one * mix_rows.astype(F32), axis=0) / gain_one
    grad_normed_one = scatter_tokens(restored(grad_rows_one))
    input_grad = grad_middle + norm_back(grad_normed_one, gain_one, scale_one, normed_one)

    small = jnp.concatenate(
        [
            gain_one_grad.reshape(shard_rows, -1),
            gain_two_grad.reshape(shard_rows, -1),
            conv_grad_local.reshape(shard_rows, -1),
        ],
        axis=1,
    )
    small = jnp.pad(small, ((0, 0), (0, 128 - small.shape[1]))).astype(BF16)
    small = jnp.broadcast_to(small, (32,) + small.shape).reshape(width, 128)
    last_grad = jnp.concatenate([grad_out_w, grad_in_w, small], axis=1)
    last_shard = exchange_sum(last_grad, FSDP)
    out_shard = last_shard[:, :chan_dev]
    in_shard = last_shard[:, chan_dev : 4 * chan_dev]
    sums = last_shard[:, 4 * chan_dev : 4 * chan_dev + 128]
    per = width // shard_rows
    conv_sum = sums[:, 2 * per : 2 * per + 3 * chan_dev // shard_rows].reshape(3, chan_dev)
    conv_sum = lax.dynamic_update_slice_in_dim(
        jnp.zeros((3, width), F32), conv_sum, tp_index * chan_dev, 1
    )
    sums = jnp.concatenate(
        [sums[:, :per].reshape(1, width), sums[:, per : 2 * per].reshape(1, width), conv_sum]
    )
    sums = no_sooner(sums, gate_part)
    sums = sums + swapped(sums, "core")
    sums = sums + swapped(sums, "yl")

    down_pair = ring_scatter(down_part.reshape(2, 4, shard_rows, -1), "x", 1, grad_in_w)
    ffn_part = jnp.concatenate(
        [gate_part.reshape(2, shard_rows, -1), down_pair.astype(BF16)], axis=2
    )
    me = lax.axis_index("yh")
    ffn_far = swapped(take(ffn_part, 0, 1 - me), "yh")
    ffn_grad_shard = take(ffn_part, 0, me).astype(F32) + ffn_far.astype(F32)
    down_shard = ffn_grad_shard[:, 2 * hidden_dev :]
    gate_shard = ffn_grad_shard[:, :hidden_dev]
    up_shard = ffn_grad_shard[:, hidden_dev : 2 * hidden_dev]
    return (
        mixed,
        input_grad,
        sums[0],
        jnp.stack([in_shard[:, i * chan_dev : (i + 1) * chan_dev] for i in range(3)]),
        sums[2:],
        out_shard.T,
        sums[1],
        jnp.stack([gate_shard, up_shard]),
        down_shard.T,
    )


def solution(mesh):
    fine = Mesh(mesh.devices.reshape(2, 4, 4, 2, 2), ALL)
    placed = (
        P(ALL, None),
        P(FSDP),
        P(),
        P(None, FSDP, TP),
        P(),
        P(TP, FSDP),
        P(),
        P(None, FSDP, TP),
        P(TP, FSDP),
        P(ALL, None),
    )
    return jax.shard_map(
        local,
        mesh=fine,
        in_specs=placed,
        out_specs=(
            P(ALL, None),
            P(ALL, None),
            P(),
            P(None, FSDP, TP),
            P(),
            P(TP, FSDP),
            P(),
            P(None, FSDP, TP),
            P(TP, FSDP),
        ),
        check_vma=False,
    )
```

profile of v0, /device:TPU:0, one launch (start us, length us, event | category | flops | bytes accessed | tf_op | source)
XLA Modules:
  0.0 277.0 jit_solution(6555508380701633619)
XLA Ops:
  11.0 3.3 %collective-permute-start.2 = (bf16[32,2176]{1,0:T(8,128)(2,1)S(1)}, bf16[32,2176]{1,0:T(8,128)(2,1)S(1)}, u32[]{:S(2)}, u32[]{:S(2)}) collective-permute-start(bf16[32,2176]{1,0:T(8,128)(2,1)S(1)} %bitcast_dynamic-update-slice_fusion.15), channel_id=1, source_target_pairs={{0,64},{64,0},{1,65},{65,1},{2,66},{66,2},{3,67},{67,3},{4,68},{68... | collective-permute-start | bytes 417800 | tf_op jit(solution)/shard_map/ppermute | solution.py:26
  23.0 2.2 collective-permute-start.4
  33.3 2.7 collective-permute-start.7
  37.1 3.9 %collective-permute-start.8 = (bf16[2,4,32,768]{3,2,1,0:T(8,128)(2,1)S(1)}, bf16[2,4,32,768]{3,2,1,0:T(8,128)(2,1)S(1)}, u32[]{:S(2)}, u32[]{:S(2)}) collective-permute-start(bf16[2,4,32,768]{3,2,1,0:T(8,128)(2,1)S(1)} %bitcast_dynamic-update-slice_fusion.14), channel_id=1, source_target_pairs={{0,8},{4,12},{8,0},{12,4},{1,9},{5,13},{9,1},{13,5},{2,10},{6,14},... | collective-permute-start | bytes 1179656 | tf_op jit(solution)/shard_map/ppermute | solution.py:22
  43.2 5.7 %collective-permute-done.6 = bf16[2,4,32,768]{3,2,1,0:T(8,128)(2,1)S(1)} collective-permute-done((bf16[2,4,32,768]{3,2,1,0:T(8,128)(2,1)S(1)}, bf16[2,4,32,768]{3,2,1,0:T(8,128)(2,1)S(1)}, u32[]{:S(2)}, u32[]{:S(2)}) %collective-permute-start.6) | collective-permute-done | bytes 393248 | tf_op jit(solution)/shard_map/ppermute | solution.py:22
  48.9 2.6 collective-permute-start.14
  51.6 2.2 collective-permute-done.7
  53.7 5.4 %collective-permute-done.8 = bf16[2,4,32,768]{3,2,1,0:T(8,128)(2,1)S(1)} collective-permute-done((bf16[2,4,32,768]{3,2,1,0:T(8,128)(2,1)S(1)}, bf16[2,4,32,768]{3,2,1,0:T(8,128)(2,1)S(1)}, u32[]{:S(2)}, u32[]{:S(2)}) %collective-permute-start.8) | collective-permute-done | bytes 393248 | tf_op jit(solution)/shard_map/ppermute | solution.py:22
  61.5 2.6 collective-permute-start.9
  66.8 4.6 %collective-permute-start.15 = (bf16[1,4,32,1408]{3,2,1,0:T(8,128)(2,1)S(1)}, bf16[1,4,32,1408]{3,2,1,0:T(8,128)(2,1)S(1)}, u32[]{:S(2)}, u32[]{:S(2)}) collective-permute-start(bf16[1,4,32,1408]{3,2,1,0:T(8,128)(2,1)S(1)} %slice.283), channel_id=1, source_target_pairs={{0,16},{16,32},{32,48},{48,0},{1,17},{17,33},{33,49},{49,1},{2,18}... | collective-permute-start | bytes 1081352 | tf_op jit(solution)/shard_map/ppermute | solution.py:22
  71.8 8.9 %collective-permute-done.15 = bf16[1,4,32,1408]{3,2,1,0:T(8,128)(2,1)S(1)} collective-permute-done((bf16[1,4,32,1408]{3,2,1,0:T(8,128)(2,1)S(1)}, bf16[1,4,32,1408]{3,2,1,0:T(8,128)(2,1)S(1)}, u32[]{:S(2)}, u32[]{:S(2)}) %collective-permute-start.15) | collective-permute-done | bytes 360480 | tf_op jit(solution)/shard_map/ppermute | solution.py:22
  80.6 3.4 %collective-permute-done.16 = bf16[1,4,32,1408]{3,2,1,0:T(8,128)(2,1)S(1)} collective-permute-done((bf16[1,4,32,1408]{3,2,1,0:T(8,128)(2,1)S(1)}, bf16[1,4,32,1408]{3,2,1,0:T(8,128)(2,1)S(1)}, u32[]{:S(2)}, u32[]{:S(2)}) %collective-permute-start.16) | collective-permute-done | bytes 360480 | tf_op jit(solution)/shard_map/ppermute | solution.py:22
  89.3 9.8 %collective-permute-done.18 = bf16[128,1024]{1,0:T(8,128)(2,1)S(1)} collective-permute-done((bf16[128,1024]{1,0:T(8,128)(2,1)S(1)}, bf16[128,1024]{1,0:T(8,128)(2,1)S(1)}, u32[]{:S(2)}, u32[]{:S(2)}) %collective-permute-start.18) | collective-permute-done | bytes 262176 | tf_op jit(solution)/shard_map/ppermute | solution.py:26
  99.8 4.9 %collective-permute-done.21 = bf16[128,1024]{0,1:T(8,128)(2,1)S(1)} collective-permute-done((bf16[128,1024]{0,1:T(8,128)(2,1)S(1)}, bf16[128,1024]{0,1:T(8,128)(2,1)S(1)}, u32[]{:S(2)}, u32[]{:S(2)}) %collective-permute-start.21) | collective-permute-done | bytes 262176 | tf_op jit(solution)/shard_map/ppermute | solution.py:26
  104.8 5.2 %collective-permute-done.19 = bf16[128,1024]{1,0:T(8,128)(2,1)S(1)} collective-permute-done((bf16[128,1024]{1,0:T(8,128)(2,1)S(1)}, bf16[128,1024]{1,0:T(8,128)(2,1)S(1)}, u32[]{:S(2)}, u32[]{:S(2)}) %collective-permute-start.19) | collective-permute-done | bytes 262176 | tf_op jit(solution)/shard_map/ppermute | solution.py:26
  110.0 6.2 %all-gather.2.cloned.1.call-done = bf16[2,1024,1152]{2,1,0:T(8,128)(2,1)} async-done(((bf16[2,32,1152]{2,1,0:T(8,128)(2,1)}), bf16[2,1024,1152]{2,1,0:T(8,128)(2,1)}) %all-gather.2.cloned.1.call-update) | async-done | bytes 4718608 | tf_op jit(solution)/shard_map/all_gather | solution.py:177
  121.9 2.4 multiply_convert_fusion
  124.3 2.9 %convolution_convert_fusion.1 = bf16[1024,1152]{1,0:T(8,128)(2,1)} fusion(bf16[512,1024]{0,1:T(8,128)(2,1)S(1)} %bitcast.219, bf16[512,1152]{1,0:T(8,128)(2,1)S(1)} %get-tuple-element.30), kind=kOutput, calls=%fused_computation.2 | convolution fusion | flops 1209139200 | bytes 4587520 | tf_op jit(solution)/shard_map/dot_general | solution.py:15
  128.9 2.9 %fusion.11 = f32[512,1024]{1,0:T(8,128)} fusion(f32[512,1024]{1,0:T(8,128)S(1)} %fusion.3, bf16[512,1152]{1,0:T(8,128)(2,1)S(1)} %get-tuple-element.51, bf16[2,1024,1152]{2,1,0:T(8,128)(2,1)S(1)} %copy-done.31), kind=kOutput, calls=%fused_computation.23 | convolution fusion | flops 1208483840 | bytes 7733248 | tf_op jit(solution)/shard_map/dot_general | solution.py:15
  133.6 5.6 %convolution_convert_fusion = bf16[1024,2304]{1,0:T(8,128)(2,1)} fusion(bf16[512,1024]{0,1:T(8,128)(2,1)S(1)} %bitcast.220, bf16[512,1152]{1,0:T(8,128)(2,1)S(1)} %copy-done.33, bf16[512,1152]{1,0:T(8,128)(2,1)} %copy-done.36), kind=kOutput, calls=%fused_computation | convolution fusion | flops 2422996992 | bytes 8126464 | tf_op jit(solution)/shard_map/dot_general | solution.py:15
  139.2 2.1 slice.415
  141.3 5.5 %all-to-all-start = ((bf16[4,256,1152]{2,1,0:T(8,128)(2,1)}), bf16[4,256,1152]{2,1,0:T(8,128)(2,1)S(1)}, u32[]{:S(2)}, u32[]{:S(2)}) async-start(bf16[4,256,1152]{2,1,0:T(8,128)(2,1)} %bitcast.209), calls=%async_computation | async-start | bytes 4718592 | tf_op jit(solution)/shard_map/all_to_all | solution.py:103
  149.0 8.0 %collective-permute-done.24 = bf16[128,1024]{1,0:T(8,128)(2,1)S(1)} collective-permute-done((bf16[128,1024]{1,0:T(8,128)(2,1)S(1)}, bf16[128,1024]{1,0:T(8,128)(2,1)S(1)}, u32[]{:S(2)}, u32[]{:S(2)}) %collective-permute-start.24) | collective-permute-done | bytes 262176 | tf_op jit(solution)/shard_map/ppermute | solution.py:26
  161.8 14.8 %all-to-all-done = bf16[4,256,1152]{2,1,0:T(8,128)(2,1)S(1)} async-done(((bf16[4,256,1152]{2,1,0:T(8,128)(2,1)}), bf16[4,256,1152]{2,1,0:T(8,128)(2,1)S(1)}, u32[]{:S(2)}, u32[]{:S(2)}) %all-to-all-start) | async-done | bytes 2359328 | tf_op jit(solution)/shard_map/all_to_all | solution.py:103
  184.9 2.4 multiply_reduce_fusion.3
  189.8 3.4 %collective-permute-done.29 = f32[2,256]{1,0:T(2,128)S(1)} collective-permute-done((f32[2,256]{1,0:T(2,128)S(1)}, f32[2,256]{1,0:T(2,128)S(1)}, u32[]{:S(2)}, u32[]{:S(2)}) %collective-permute-start.29) | collective-permute-done | bytes 2080 | tf_op jit(solution)/shard_map/ppermute | solution.py:150
  193.4 4.0 %multiply_reduce_fusion = (f32[1024]{0:T(1024)S(1)}, f32[512,1024]{1,0:T(8,128)}) fusion(bf16[128,1024]{1,0:T(8,128)(2,1)S(1)} %copy-done.22, bf16[128,1024]{1,0:T(8,128)(2,1)S(1)} %copy-done.24, bf16[128,1024]{1,0:T(8,128)(2,1)} %copy-done.25, bf16[128,1024]{1,0:T(8,128)(2,1)S(1)} %copy-done.20, bf16[1024,768]{1,0:T(8,128)(2,1)} %bitcast.213, ...), kind=kOutput, calls=%fused_computation.13 | convolution fusion | flops 812907520 | bytes 5509120 | tf_op jit(solution)/shard_map/dot_general | solution.py:15
  202.6 9.5 %all-to-all-start.1 = ((bf16[32,32,1152]{2,1,0:T(8,128)(2,1)}), bf16[32,32,1152]{2,1,0:T(8,128)(2,1)S(1)}, u32[]{:S(2)}, u32[]{:S(2)}) async-start(bf16[32,32,1152]{2,1,0:T(8,128)(2,1)} %pad_maximum_fusion), calls=%async_computation.1 | async-start | bytes 4718592 | tf_op jit(solution)/shard_map/all_to_all | solution.py:103
  227.9 16.3 %collective-permute-done.34 = bf16[2,32,1152]{2,1,0:T(8,128)(2,1)S(1)} collective-permute-done((bf16[2,32,1152]{2,1,0:T(8,128)(2,1)S(1)}, bf16[2,32,1152]{2,1,0:T(8,128)(2,1)S(1)}, u32[]{:S(2)}, u32[]{:S(2)}) %collective-permute-start.34) | collective-permute-done | bytes 147488 | tf_op jit(solution)/shard_map/ppermute | solution.py:22
  244.3 3.0 %collective-permute-done.36 = bf16[2,32,1152]{2,1,0:T(8,128)(2,1)S(1)} collective-permute-done((bf16[2,32,1152]{2,1,0:T(8,128)(2,1)S(1)}, bf16[2,32,1152]{2,1,0:T(8,128)(2,1)S(1)}, u32[]{:S(2)}, u32[]{:S(2)}) %collective-permute-start.36) | collective-permute-done | bytes 147488 | tf_op jit(solution)/shard_map/ppermute | solution.py:22
  251.0 3.7 %reduce-scatter.5.cloned.1.call-done = bf16[64,2304]{1,0:T(8,128)(2,1)} async-done(((bf16[256,2304]{1,0:T(8,128)(2,1)}), bf16[64,2304]{1,0:T(8,128)(2,1)}) %reduce-scatter.5.cloned.1.call-update) | async-done | bytes 294928 | tf_op jit(solution)/shard_map/reduce_scatter | solution.py:231
  263.0 5.1 %collective-permute-done.37 = bf16[32,3456]{1,0:T(8,128)(2,1)S(1)} collective-permute-done((bf16[32,3456]{1,0:T(8,128)(2,1)S(1)}, bf16[32,3456]{1,0:T(8,128)(2,1)S(1)}, u32[]{:S(2)}, u32[]{:S(2)}) %collective-permute-start.37) | collective-permute-done | bytes 221216 | tf_op jit(solution)/shard_map/ppermute | solution.py:26
  (273 shorter events, 94.9 us)
Async XLA Ops:
  7.2 109.0 %all-gather.2.cloned.1.call-start = ((), (), s32[]{:S(2)}) async-start(), calls=%async_computation.4 | async-start | bytes 4866048 | tf_op jit(solution)/shard_map/all_gather | solution.py:177
  11.0 9.9 %collective-permute-start.2 = (bf16[32,2176]{1,0:T(8,128)(2,1)S(1)}, bf16[32,2176]{1,0:T(8,128)(2,1)S(1)}, u32[]{:S(2)}, u32[]{:S(2)}) collective-permute-start(bf16[32,2176]{1,0:T(8,128)(2,1)S(1)} %bitcast_dynamic-update-slice_fusion.15), channel_id=1, source_target_pairs={{0,64},{64,0},{1,65},{65,1},{2,66},{66,2},{3,67},{67,3},{4,68},{68... | collective-permute-start | bytes 417800 | tf_op jit(solution)/shard_map/ppermute | solution.py:26
  17.2 16.1 %collective-permute-start = (bf16[128,1024]{1,0:T(8,128)(2,1)S(1)}, bf16[128,1024]{1,0:T(8,128)(2,1)S(1)}, u32[]{:S(2)}, u32[]{:S(2)}) collective-permute-start(bf16[128,1024]{1,0:T(8,128)(2,1)S(1)} %fusion.20), channel_id=1, source_target_pairs={{0,2},{2,0},{1,3},{3,1},{4,6},{6,4},{5,7},{7,5},{8,10},{10,8},{9,1... | collective-permute-start | bytes 786440 | tf_op jit(solution)/shard_map/ppermute | solution.py:26
  18.0 199.9 %reduce-scatter.3.cloned.1.call-start = ((), (), s32[]{:S(2)}) async-start(), calls=%async_computation.5 | async-start | bytes 5898240 | tf_op jit(solution)/shard_map/reduce_scatter | solution.py:230
  27.1 10.0 %collective-permute-start.10 = (bf16[2,32,1408]{2,1,0:T(8,128)(2,1)S(1)}, bf16[2,32,1408]{2,1,0:T(8,128)(2,1)S(1)}, u32[]{:S(2)}, u32[]{:S(2)}) collective-permute-start(bf16[2,32,1408]{2,1,0:T(8,128)(2,1)S(1)} %get-tuple-element.50), channel_id=1, source_target_pairs={{0,4},{4,8},{8,12},{12,0},{1,5},{5,9},{9,13},{13,1},{2,6},{6,10},{... | collective-permute-start | bytes 540680 | tf_op jit(solution)/shard_map/ppermute | solution.py:22
  28.7 12.4 %collective-permute-start.11 = (bf16[2,32,1408]{2,1,0:T(8,128)(2,1)S(1)}, bf16[2,32,1408]{2,1,0:T(8,128)(2,1)S(1)}, u32[]{:S(2)}, u32[]{:S(2)}) collective-permute-start(bf16[2,32,1408]{2,1,0:T(8,128)(2,1)S(1)} %get-tuple-element.50), channel_id=1, source_target_pairs={{0,12},{4,0},{8,4},{12,8},{1,13},{5,1},{9,5},{13,9},{2,14},{6,2},{... | collective-permute-start | bytes 540680 | tf_op jit(solution)/shard_map/ppermute | solution.py:22
  30.5 11.3 %collective-permute-start.12 = (bf16[2,32,1408]{2,1,0:T(8,128)(2,1)S(1)}, bf16[2,32,1408]{2,1,0:T(8,128)(2,1)S(1)}, u32[]{:S(2)}, u32[]{:S(2)}) collective-permute-start(bf16[2,32,1408]{2,1,0:T(8,128)(2,1)S(1)} %get-tuple-element.50), channel_id=1, source_target_pairs={{0,8},{4,12},{8,0},{12,4},{1,9},{5,13},{9,1},{13,5},{2,10},{6,14},... | collective-permute-start | bytes 540680 | tf_op jit(solution)/shard_map/ppermute | solution.py:22
  32.4 16.5 %collective-permute-start.6 = (bf16[2,4,32,768]{3,2,1,0:T(8,128)(2,1)S(1)}, bf16[2,4,32,768]{3,2,1,0:T(8,128)(2,1)S(1)}, u32[]{:S(2)}, u32[]{:S(2)}) collective-permute-start(bf16[2,4,32,768]{3,2,1,0:T(8,128)(2,1)S(1)} %bitcast_dynamic-update-slice_fusion.14), channel_id=1, source_target_pairs={{0,4},{4,8},{8,12},{12,0},{1,5},{5,9},{9,13},{13,1},{2,6},{6,10},{... | collective-permute-start | bytes 1179656 | tf_op jit(solution)/shard_map/ppermute | solution.py:22
  33.3 20.4 %collective-permute-start.7 = (bf16[2,4,32,768]{3,2,1,0:T(8,128)(2,1)S(1)}, bf16[2,4,32,768]{3,2,1,0:T(8,128)(2,1)S(1)}, u32[]{:S(2)}, u32[]{:S(2)}) collective-permute-start(bf16[2,4,32,768]{3,2,1,0:T(8,128)(2,1)S(1)} %bitcast_dynamic-update-slice_fusion.14), channel_id=1, source_target_pairs={{0,12},{4,0},{8,4},{12,8},{1,13},{5,1},{9,5},{13,9},{2,14},{6,2},{... | collective-permute-start | bytes 1179656 | tf_op jit(solution)/shard_map/ppermute | solution.py:22
  37.1 22.0 %collective-permute-start.8 = (bf16[2,4,32,768]{3,2,1,0:T(8,128)(2,1)S(1)}, bf16[2,4,32,768]{3,2,1,0:T(8,128)(2,1)S(1)}, u32[]{:S(2)}, u32[]{:S(2)}) collective-permute-start(bf16[2,4,32,768]{3,2,1,0:T(8,128)(2,1)S(1)} %bitcast_dynamic-update-slice_fusion.14), channel_id=1, source_target_pairs={{0,8},{4,12},{8,0},{12,4},{1,9},{5,13},{9,1},{13,5},{2,10},{6,14},... | collective-permute-start | bytes 1179656 | tf_op jit(solution)/shard_map/ppermute | solution.py:22
  41.1 18.1 %collective-permute-start.1 = (bf16[256,1024]{1,0:T(8,128)(2,1)S(1)}, bf16[256,1024]{1,0:T(8,128)(2,1)S(1)}, u32[]{:S(2)}, u32[]{:S(2)}) collective-permute-start(bf16[256,1024]{1,0:T(8,128)(2,1)S(1)} %pad_maximum_fusion.9), channel_id=1, source_target_pairs={{0,1},{1,0},{2,3},{3,2},{4,5},{5,4},{6,7},{7,6},{8,9},{9,8},{10,11... | collective-permute-start | bytes 1572872 | tf_op jit(solution)/shard_map/ppermute | solution.py:26
  41.9 24.9 %collective-permute-start.13 = (bf16[2,4,32,1408]{3,2,1,0:T(8,128)(2,1)S(1)}, bf16[2,4,32,1408]{3,2,1,0:T(8,128)(2,1)S(1)}, u32[]{:S(2)}, u32[]{:S(2)}) collective-permute-start(bf16[2,4,32,1408]{3,2,1,0:T(8,128)(2,1)S(1)} %bitcast_dynamic-update-slice_fusion.7), channel_id=1, source_target_pairs={{0,16},{16,32},{32,48},{48,0},{1,17},{17,33},{33,49},{49,1},{2,18}... | collective-permute-start | bytes 2162696 | tf_op jit(solution)/shard_map/ppermute | solution.py:22
  48.9 22.5 %collective-permute-start.14 = (bf16[2,4,32,1408]{3,2,1,0:T(8,128)(2,1)S(1)}, bf16[2,4,32,1408]{3,2,1,0:T(8,128)(2,1)S(1)}, u32[]{:S(2)}, u32[]{:S(2)}) collective-permute-start(bf16[2,4,32,1408]{3,2,1,0:T(8,128)(2,1)S(1)} %bitcast_dynamic-update-slice_fusion.7), channel_id=1, source_target_pairs={{0,48},{16,0},{32,16},{48,32},{1,49},{17,1},{33,17},{49,33},{2,50}... | collective-permute-start | bytes 2162696 | tf_op jit(solution)/shard_map/ppermute | solution.py:22
  66.8 13.8 %collective-permute-start.15 = (bf16[1,4,32,1408]{3,2,1,0:T(8,128)(2,1)S(1)}, bf16[1,4,32,1408]{3,2,1,0:T(8,128)(2,1)S(1)}, u32[]{:S(2)}, u32[]{:S(2)}) collective-permute-start(bf16[1,4,32,1408]{3,2,1,0:T(8,128)(2,1)S(1)} %slice.283), channel_id=1, source_target_pairs={{0,16},{16,32},{32,48},{48,0},{1,17},{17,33},{33,49},{49,1},{2,18}... | collective-permute-start | bytes 1081352 | tf_op jit(solution)/shard_map/ppermute | solution.py:22
  71.4 12.6 %collective-permute-start.16 = (bf16[1,4,32,1408]{3,2,1,0:T(8,128)(2,1)S(1)}, bf16[1,4,32,1408]{3,2,1,0:T(8,128)(2,1)S(1)}, u32[]{:S(2)}, u32[]{:S(2)}) collective-permute-start(bf16[1,4,32,1408]{3,2,1,0:T(8,128)(2,1)S(1)} %slice.284), channel_id=1, source_target_pairs={{0,48},{16,0},{32,16},{48,32},{1,49},{17,1},{33,17},{49,33},{2,50}... | collective-permute-start | bytes 1081352 | tf_op jit(solution)/shard_map/ppermute | solution.py:22
  86.9 12.2 %collective-permute-start.18 = (bf16[128,1024]{1,0:T(8,128)(2,1)S(1)}, bf16[128,1024]{1,0:T(8,128)(2,1)S(1)}, u32[]{:S(2)}, u32[]{:S(2)}) collective-permute-start(bf16[128,1024]{1,0:T(8,128)(2,1)S(1)} %slice.420), channel_id=1, source_target_pairs={{0,2},{2,0},{1,3},{3,1},{4,6},{6,4},{5,7},{7,5},{8,10},{10,8},{9,1... | collective-permute-start | bytes 786440 | tf_op jit(solution)/shard_map/ppermute | solution.py:26
  88.2 16.5 %collective-permute-start.21 = (bf16[128,1024]{0,1:T(8,128)(2,1)S(1)}, bf16[128,1024]{0,1:T(8,128)(2,1)S(1)}, u32[]{:S(2)}, u32[]{:S(2)}) collective-permute-start(bf16[128,1024]{0,1:T(8,128)(2,1)S(1)} %copy.38), channel_id=1, source_target_pairs={{0,2},{2,0},{1,3},{3,1},{4,6},{6,4},{5,7},{7,5},{8,10},{10,8},{9,1... | collective-permute-start | bytes 786440 | tf_op jit(solution)/shard_map/ppermute | solution.py:26
  99.4 10.6 %collective-permute-start.19 = (bf16[128,1024]{1,0:T(8,128)(2,1)S(1)}, bf16[128,1024]{1,0:T(8,128)(2,1)S(1)}, u32[]{:S(2)}, u32[]{:S(2)}) collective-permute-start(bf16[128,1024]{1,0:T(8,128)(2,1)S(1)} %multiply_convert_fusion.4), channel_id=1, source_target_pairs={{0,2},{2,0},{1,3},{3,1},{4,6},{6,4},{5,7},{7,5},{8,10},{10,8},{9,1... | collective-permute-start | bytes 786440 | tf_op jit(solution)/shard_map/ppermute | solution.py:26
  104.8 11.8 %collective-permute-start.22 = (bf16[256,1024]{0,1:T(8,128)(2,1)S(1)}, bf16[256,1024]{0,1:T(8,128)(2,1)S(1)}, u32[]{:S(2)}, u32[]{:S(2)}) collective-permute-start(bf16[256,1024]{0,1:T(8,128)(2,1)S(1)} %pad_maximum_fusion.11), channel_id=1, source_target_pairs={{0,1},{1,0},{2,3},{3,2},{4,5},{5,4},{6,7},{7,6},{8,9},{9,8},{10,11... | collective-permute-start | bytes 1572872 | tf_op jit(solution)/shard_map/ppermute | solution.py:26
  141.3 35.3 %all-to-all-start = ((bf16[4,256,1152]{2,1,0:T(8,128)(2,1)}), bf16[4,256,1152]{2,1,0:T(8,128)(2,1)S(1)}, u32[]{:S(2)}, u32[]{:S(2)}) async-start(bf16[4,256,1152]{2,1,0:T(8,128)(2,1)} %bitcast.209), calls=%async_computation | async-start | bytes 4718592 | tf_op jit(solution)/shard_map/all_to_all | solution.py:103
  148.6 8.4 %collective-permute-start.24 = (bf16[128,1024]{1,0:T(8,128)(2,1)S(1)}, bf16[128,1024]{1,0:T(8,128)(2,1)S(1)}, u32[]{:S(2)}, u32[]{:S(2)}) collective-permute-start(bf16[128,1024]{1,0:T(8,128)(2,1)S(1)} %slice.419), channel_id=1, source_target_pairs={{0,2},{2,0},{1,3},{3,1},{4,6},{6,4},{5,7},{7,5},{8,10},{10,8},{9,1... | collective-permute-start | bytes 786440 | tf_op jit(solution)/shard_map/ppermute | solution.py:26
  158.3 21.5 %collective-permute-start.25 = (bf16[128,1024]{1,0:T(8,128)(2,1)S(1)}, bf16[128,1024]{1,0:T(8,128)(2,1)}, u32[]{:S(2)}, u32[]{:S(2)}) collective-permute-start(bf16[128,1024]{1,0:T(8,128)(2,1)S(1)} %get-tuple-element.39), channel_id=1, source_target_pairs={{0,2},{2,0},{1,3},{3,1},{4,6},{6,4},{5,7},{7,5},{8,10},{10,8},{9,1... | collective-permute-start | bytes 786440 | tf_op jit(solution)/shard_map/ppermute | solution.py:26
  161.8 19.2 %collective-permute-start.27 = (bf16[256,1024]{1,0:T(8,128)(2,1)}, bf16[256,1024]{1,0:T(8,128)(2,1)}, u32[]{:S(2)}, u32[]{:S(2)}) collective-permute-start(bf16[256,1024]{1,0:T(8,128)(2,1)} %slice.414), channel_id=1, source_target_pairs={{0,1},{1,0},{2,3},{3,2},{4,5},{5,4},{6,7},{7,6},{8,9},{9,8},{10,11... | collective-permute-start | bytes 1572872 | tf_op jit(solution)/shard_map/ppermute | solution.py:26
  183.4 30.9 %collective-permute-start.28 = (bf16[128,1024]{1,0:T(8,128)(2,1)}, bf16[128,1024]{1,0:T(8,128)(2,1)}, u32[]{:S(2)}, u32[]{:S(2)}) collective-permute-start(bf16[128,1024]{1,0:T(8,128)(2,1)} %slice.418), channel_id=1, source_target_pairs={{0,2},{2,0},{1,3},{3,1},{4,6},{6,4},{5,7},{7,5},{8,10},{10,8},{9,1... | collective-permute-start | bytes 786440 | tf_op jit(solution)/shard_map/ppermute | solution.py:26
  202.6 47.0 %all-to-all-start.1 = ((bf16[32,32,1152]{2,1,0:T(8,128)(2,1)}), bf16[32,32,1152]{2,1,0:T(8,128)(2,1)S(1)}, u32[]{:S(2)}, u32[]{:S(2)}) async-start(bf16[32,32,1152]{2,1,0:T(8,128)(2,1)} %pad_maximum_fusion), calls=%async_computation.1 | async-start | bytes 4718592 | tf_op jit(solution)/shard_map/all_to_all | solution.py:103
  212.1 42.6 %reduce-scatter.5.cloned.1.call-start = ((), (), s32[]{:S(2)}) async-start(), calls=%async_computation.6 | async-start | bytes 1474560 | tf_op jit(solution)/shard_map/reduce_scatter | solution.py:231
  214.3 11.4 %collective-permute-start.30 = (bf16[256,1024]{1,0:T(8,128)(2,1)}, bf16[256,1024]{1,0:T(8,128)(2,1)}, u32[]{:S(2)}, u32[]{:S(2)}) collective-permute-start(bf16[256,1024]{1,0:T(8,128)(2,1)} %pad_maximum_fusion.13), channel_id=1, source_target_pairs={{0,1},{1,0},{2,3},{3,2},{4,5},{5,4},{6,7},{7,6},{8,9},{9,8},{10,11... | collective-permute-start | bytes 1572872 | tf_op jit(solution)/shard_map/ppermute | solution.py:26
  219.1 25.2 %collective-permute-start.34 = (bf16[2,32,1152]{2,1,0:T(8,128)(2,1)S(1)}, bf16[2,32,1152]{2,1,0:T(8,128)(2,1)S(1)}, u32[]{:S(2)}, u32[]{:S(2)}) collective-permute-start(bf16[2,32,1152]{2,1,0:T(8,128)(2,1)S(1)} %get-tuple-element.68), channel_id=1, source_target_pairs={{0,4},{4,8},{8,12},{12,0},{1,5},{5,9},{9,13},{13,1},{2,6},{6,10},{... | collective-permute-start | bytes 442376 | tf_op jit(solution)/shard_map/ppermute | solution.py:22
  220.9 23.3 %collective-permute-start.35 = (bf16[2,32,1152]{2,1,0:T(8,128)(2,1)S(1)}, bf16[2,32,1152]{2,1,0:T(8,128)(2,1)S(1)}, u32[]{:S(2)}, u32[]{:S(2)}) collective-permute-start(bf16[2,32,1152]{2,1,0:T(8,128)(2,1)S(1)} %get-tuple-element.69), channel_id=1, source_target_pairs={{0,12},{4,0},{8,4},{12,8},{1,13},{5,1},{9,5},{13,9},{2,14},{6,2},{... | collective-permute-start | bytes 442376 | tf_op jit(solution)/shard_map/ppermute | solution.py:22
  222.4 24.9 %collective-permute-start.36 = (bf16[2,32,1152]{2,1,0:T(8,128)(2,1)S(1)}, bf16[2,32,1152]{2,1,0:T(8,128)(2,1)S(1)}, u32[]{:S(2)}, u32[]{:S(2)}) collective-permute-start(bf16[2,32,1152]{2,1,0:T(8,128)(2,1)S(1)} %get-tuple-element.70), channel_id=1, source_target_pairs={{0,8},{4,12},{8,0},{12,4},{1,9},{5,13},{9,1},{13,5},{2,10},{6,14},... | collective-permute-start | bytes 442376 | tf_op jit(solution)/shard_map/ppermute | solution.py:22
  227.1 21.2 %collective-permute-start.31 = (bf16[128,1024]{1,0:T(8,128)(2,1)S(1)}, bf16[128,1024]{1,0:T(8,128)(2,1)S(1)}, u32[]{:S(2)}, u32[]{:S(2)}) collective-permute-start(bf16[128,1024]{1,0:T(8,128)(2,1)S(1)} %slice.417), channel_id=1, source_target_pairs={{0,2},{2,0},{1,3},{3,1},{4,6},{6,4},{5,7},{7,5},{8,10},{10,8},{9,1... | collective-permute-start | bytes 786440 | tf_op jit(solution)/shard_map/ppermute | solution.py:26
  259.3 8.8 %collective-permute-start.37 = (bf16[32,3456]{1,0:T(8,128)(2,1)S(1)}, bf16[32,3456]{1,0:T(8,128)(2,1)S(1)}, u32[]{:S(2)}, u32[]{:S(2)}) collective-permute-start(bf16[32,3456]{1,0:T(8,128)(2,1)S(1)} %fusion.47), channel_id=1, source_target_pairs={{0,64},{64,0},{1,65},{65,1},{2,66},{66,2},{3,67},{67,3},{4,68},{68... | collective-permute-start | bytes 663560 | tf_op jit(solution)/shard_map/ppermute | solution.py:26
  (49 other events, 211.5 us)
Sparse Core Ops, SparseCore 0:
  18.1 98.0 all-gather.1
  139.3 49.4 reduce-scatter.2
  218.1 36.5 reduce-scatter.4
where the time goes:
time: 279 us; the launch traced here: 277 us
  waiting for transfers between devices  113 us (41%)
  starting transfers between devices  63.4 us (23%)
  matrix products  30.4 us (11%)
  other arithmetic  28.1 us (10%)
  local copies, waits for them, and re-layouts  24.9 us (9%)
  between operations  17 us (6%)
    ppermute x16, waiting for transfers between devices, shifted(): lax.ppermute(value, axis, [(i, (i + by) % size) for i in range(size)])  46.6 us
    ppermute x20, waiting for transfers between devices, swapped(): return lax.ppermute(value, axis, [(0, 1), (1, 0)])  37.7 us
    ppermute x16, starting transfers between devices, shifted(): lax.ppermute(value, axis, [(i, (i + by) % size) for i in range(size)])  32.5 us
    dot_general x14, matrix products, dot(): lax.dot_general(lhs, rhs, (((lhs_dim,), (rhs_dim,)), ((), ())), preferred...  30.4 us
    all_to_all x2, starting transfers between devices, exchange_sum(): parts = lax.all_to_all(whole.reshape(count, -1, whole.shape[1]), axes, 0, 0)  15 us
    all_to_all x2, waiting for transfers between devices, exchange_sum(): parts = lax.all_to_all(whole.reshape(count, -1, whole.shape[1]), axes, 0, 0)  14.8 us
    ppermute x20, starting transfers between devices, swapped(): return lax.ppermute(value, axis, [(0, 1), (1, 0)])  11.8 us
    unnamed x80, local copies, waits for them, and re-layouts  8.32 us
  transfers between devices with their start and end apart: 43, of which 23 were waited for; matrix products, arithmetic and copies ran while one was open for 19% of the time, Pallas kernels for 0%

commit v1 on v0

--- a/solution.py
+++ b/solution.py
@@ -79,8 +79,7 @@
     return jnp.stack([jnp.where(first, shard, other), jnp.where(first, other, shard)])
 
 
-def gather_rows(first, second):
-    pair = pair_rows(jnp.concatenate([first, second], axis=1))
+def gather_rows(first, second, pair):
     columns = first.shape[1]
     one = ring_gather(ring_gather(pair[:, :, :columns], "z", 1), "x", 2)
     two = ring_gather_passing(ring_gather(pair[:, :, columns:], "x", 1), "z", 1)
@@ -169,15 +168,15 @@
     tp_index = lax.axis_index("yl") * 2 + lax.axis_index("core")
 
     in_shard = jnp.concatenate([in_weight[0], in_weight[1], in_weight[2]], axis=1)
-    in_full, second_full = gather_rows(
-        in_shard, jnp.concatenate([out_weight.T, down_weight.T], axis=1)
-    )
+    second_shard = jnp.concatenate([out_weight.T, down_weight.T], axis=1)
+    mixer_pair = pair_rows(jnp.concatenate([in_shard, second_shard], axis=1))
+    in_full, second_full = gather_rows(in_shard, second_shard, mixer_pair)
     out_full = second_full[:, :chan_dev]
     down_full = second_full[:, chan_dev:]
     up_gate_full = lax.all_gather(up_gate_weight, FSDP, axis=1, tiled=True)
 
     conv_local = lax.dynamic_slice_in_dim(conv_weight, tp_index * chan_dev, chan_dev, 1).astype(F32)
-    tok_f32 = tokens.astype(F32)
+    tok_f32 = no_sooner(tokens, mixer_pair).astype(F32)
     scale_one, normed_one = norm_parts(tok_f32)
     gain_one = mix_gain.astype(F32)
     mix_rows = reordered(gather_tokens((normed_one * gain_one).astype(BF16)))

time: 279 us -> 270 us (0.968)
  waiting for transfers between devices: 113 us -> 107 us
    all_gather x1, waiting for transfers between devices: 6.16 us -> 0.01 us  [local(): up_gate_full = lax.all_gather(up_gate_weight, FSDP, axis=1, tiled=True)]
    ppermute x16, starting transfers between devices: 32.5 us -> 27.5 us  [shifted(): lax.ppermute(value, axis, [(i, (i + by) % size) for i in range(size)])]
    ppermute x16, waiting for transfers between devices: 46.6 us -> 50.6 us  [shifted(): lax.ppermute(value, axis, [(i, (i + by) % size) for i in range(size)])]
    ppermute x20, waiting for transfers between devices: 37.7 us -> 34.5 us  [swapped(): return lax.ppermute(value, axis, [(0, 1), (1, 0)])]
  transfers between devices with their start and end apart: 43 -> 43, of which waited for: 23 -> 22; matrix products, arithmetic and copies ran while one was open for 19% -> 19% of each run, Pallas kernels for 0% -> 0%
where the time goes in v1:
time: 270 us; the launch traced here: 269 us
  waiting for transfers between devices  107 us (40%)
  starting transfers between devices  62.4 us (23%)
  matrix products  30.4 us (11%)
  other arithmetic  26 us (10%)
  local copies, waits for them, and re-layouts  25.1 us (9%)
  between operations  17.7 us (7%)
    ppermute x16, waiting for transfers between devices, shifted(): lax.ppermute(value, axis, [(i, (i + by) % size) for i in range(size)])  50.6 us
    ppermute x20, waiting for transfers between devices, swapped(): return lax.ppermute(value, axis, [(0, 1), (1, 0)])  34.5 us
    dot_general x14, matrix products, dot(): lax.dot_general(lhs, rhs, (((lhs_dim,), (rhs_dim,)), ((), ())), preferred...  30.4 us
    ppermute x16, starting transfers between devices, shifted(): lax.ppermute(value, axis, [(i, (i + by) % size) for i in range(size)])  27.5 us
    all_to_all x2, starting transfers between devices, exchange_sum(): parts = lax.all_to_all(whole.reshape(count, -1, whole.shape[1]), axes, 0, 0)  15.7 us
    all_to_all x2, waiting for transfers between devices, exchange_sum(): parts = lax.all_to_all(whole.reshape(count, -1, whole.shape[1]), axes, 0, 0)  14.8 us
    ppermute x20, starting transfers between devices, swapped(): return lax.ppermute(value, axis, [(0, 1), (1, 0)])  14.1 us
    unnamed x80, local copies, waits for them, and re-layouts  8 us
  transfers between devices with their start and end apart: 43, of which 22 were waited for; matrix products, arithmetic and copies ran while one was open for 19% of the time, Pallas kernels for 0%

profile of v1, /device:TPU:0, one launch (start us, length us, event | category | flops | bytes accessed | tf_op | source)
XLA Modules:
  0.0 268.7 jit_solution(3052520504558502824)
XLA Ops:
  11.0 3.3 %collective-permute-start = (bf16[32,2176]{1,0:T(8,128)(2,1)S(1)}, bf16[32,2176]{1,0:T(8,128)(2,1)S(1)}, u32[]{:S(2)}, u32[]{:S(2)}) collective-permute-start(bf16[32,2176]{1,0:T(8,128)(2,1)S(1)} %bitcast_dynamic-update-slice_fusion.15), channel_id=1, source_target_pairs={{0,64},{64,0},{1,65},{65,1},{2,66},{66,2},{3,67},{67,3},{4,68},{68... | collective-permute-start | bytes 417800 | tf_op jit(solution)/shard_map/ppermute | solution.py:26
  18.2 2.0 collective-permute-start.3
  20.2 2.2 collective-permute-start.4
  33.6 2.7 %collective-permute-start.7 = (bf16[2,4,32,768]{3,2,1,0:T(8,128)(2,1)S(1)}, bf16[2,4,32,768]{3,2,1,0:T(8,128)(2,1)S(1)}, u32[]{:S(2)}, u32[]{:S(2)}) collective-permute-start(bf16[2,4,32,768]{3,2,1,0:T(8,128)(2,1)S(1)} %bitcast_dynamic-update-slice_fusion.14), channel_id=1, source_target_pairs={{0,12},{4,0},{8,4},{12,8},{1,13},{5,1},{9,5},{13,9},{2,14},{6,2},{... | collective-permute-start | bytes 1179656 | tf_op jit(solution)/shard_map/ppermute | solution.py:22
  40.0 2.1 collective-permute-start.14
  42.2 4.6 %collective-permute-done.6 = bf16[2,4,32,768]{3,2,1,0:T(8,128)(2,1)S(1)} collective-permute-done((bf16[2,4,32,768]{3,2,1,0:T(8,128)(2,1)S(1)}, bf16[2,4,32,768]{3,2,1,0:T(8,128)(2,1)S(1)}, u32[]{:S(2)}, u32[]{:S(2)}) %collective-permute-start.6) | collective-permute-done | bytes 393248 | tf_op jit(solution)/shard_map/ppermute | solution.py:22
  48.2 9.1 %collective-permute-done.8 = bf16[2,4,32,768]{3,2,1,0:T(8,128)(2,1)S(1)} collective-permute-done((bf16[2,4,32,768]{3,2,1,0:T(8,128)(2,1)S(1)}, bf16[2,4,32,768]{3,2,1,0:T(8,128)(2,1)S(1)}, u32[]{:S(2)}, u32[]{:S(2)}) %collective-permute-start.8) | collective-permute-done | bytes 393248 | tf_op jit(solution)/shard_map/ppermute | solution.py:22
  59.7 3.6 %collective-permute-start.9 = (f32[3,256]{1,0:T(4,128)S(1)}, f32[3,256]{1,0:T(4,128)S(1)}, u32[]{:S(2)}, u32[]{:S(2)}) collective-permute-start(f32[3,256]{1,0:T(4,128)S(1)} %select_maximum_fusion), channel_id=1, source_target_pairs={{0,4},{4,8},{8,12},{12,16},{16,20},{20,24},{24,28},{28,32},{32,36}... | collective-permute-start | bytes 9224 | tf_op jit(solution)/shard_map/ppermute | solution.py:149
  66.0 3.4 %collective-permute-start.15 = (bf16[1,4,32,1408]{3,2,1,0:T(8,128)(2,1)S(1)}, bf16[1,4,32,1408]{3,2,1,0:T(8,128)(2,1)S(1)}, u32[]{:S(2)}, u32[]{:S(2)}) collective-permute-start(bf16[1,4,32,1408]{3,2,1,0:T(8,128)(2,1)S(1)} %slice.288), channel_id=1, source_target_pairs={{0,16},{16,32},{32,48},{48,0},{1,17},{17,33},{33,49},{49,1},{2,18}... | collective-permute-start | bytes 1081352 | tf_op jit(solution)/shard_map/ppermute | solution.py:22
  69.7 11.1 %collective-permute-done.15 = bf16[1,4,32,1408]{3,2,1,0:T(8,128)(2,1)S(1)} collective-permute-done((bf16[1,4,32,1408]{3,2,1,0:T(8,128)(2,1)S(1)}, bf16[1,4,32,1408]{3,2,1,0:T(8,128)(2,1)S(1)}, u32[]{:S(2)}, u32[]{:S(2)}) %collective-permute-start.15) | collective-permute-done | bytes 360480 | tf_op jit(solution)/shard_map/ppermute | solution.py:22
  80.8 2.3 collective-permute-done.16
  88.4 6.9 %collective-permute-done.18 = bf16[128,1024]{1,0:T(8,128)(2,1)S(1)} collective-permute-done((bf16[128,1024]{1,0:T(8,128)(2,1)S(1)}, bf16[128,1024]{1,0:T(8,128)(2,1)S(1)}, u32[]{:S(2)}, u32[]{:S(2)}) %collective-permute-start.18) | collective-permute-done | bytes 262176 | tf_op jit(solution)/shard_map/ppermute | solution.py:26
  96.6 4.3 %collective-permute-done.21 = bf16[128,1024]{0,1:T(8,128)(2,1)S(1)} collective-permute-done((bf16[128,1024]{0,1:T(8,128)(2,1)S(1)}, bf16[128,1024]{0,1:T(8,128)(2,1)S(1)}, u32[]{:S(2)}, u32[]{:S(2)}) %collective-permute-start.21) | collective-permute-done | bytes 262176 | tf_op jit(solution)/shard_map/ppermute | solution.py:26
  101.0 5.0 %collective-permute-done.19 = bf16[128,1024]{1,0:T(8,128)(2,1)S(1)} collective-permute-done((bf16[128,1024]{1,0:T(8,128)(2,1)S(1)}, bf16[128,1024]{1,0:T(8,128)(2,1)S(1)}, u32[]{:S(2)}, u32[]{:S(2)}) %collective-permute-start.19) | collective-permute-done | bytes 262176 | tf_op jit(solution)/shard_map/ppermute | solution.py:26
  111.7 2.4 multiply_convert_fusion
  114.2 2.9 %convolution_convert_fusion.1 = bf16[1024,1152]{1,0:T(8,128)(2,1)} fusion(bf16[512,1024]{0,1:T(8,128)(2,1)S(1)} %bitcast.220, bf16[512,1152]{1,0:T(8,128)(2,1)S(1)} %get-tuple-element.30), kind=kOutput, calls=%fused_computation.2 | convolution fusion | flops 1209139200 | bytes 4587520 | tf_op jit(solution)/shard_map/dot_general | solution.py:15
  118.7 2.9 %fusion.11 = f32[512,1024]{1,0:T(8,128)} fusion(f32[512,1024]{1,0:T(8,128)S(1)} %fusion.3, bf16[512,1152]{1,0:T(8,128)(2,1)S(1)} %get-tuple-element.51, bf16[2,1024,1152]{2,1,0:T(8,128)(2,1)S(1)} %copy-done.31), kind=kOutput, calls=%fused_computation.23 | convolution fusion | flops 1208483840 | bytes 7733248 | tf_op jit(solution)/shard_map/dot_general | solution.py:15
  123.5 5.6 %convolution_convert_fusion = bf16[1024,2304]{1,0:T(8,128)(2,1)} fusion(bf16[512,1024]{0,1:T(8,128)(2,1)S(1)} %bitcast.221, bf16[512,1152]{1,0:T(8,128)(2,1)S(1)} %copy-done.33, bf16[512,1152]{1,0:T(8,128)(2,1)} %copy-done.36), kind=kOutput, calls=%fused_computation | convolution fusion | flops 2422996992 | bytes 8126464 | tf_op jit(solution)/shard_map/dot_general | solution.py:15
  129.0 2.1 slice.420
  131.2 4.4 %all-to-all-start = ((bf16[4,256,1152]{2,1,0:T(8,128)(2,1)}), bf16[4,256,1152]{2,1,0:T(8,128)(2,1)S(1)}, u32[]{:S(2)}, u32[]{:S(2)}) async-start(bf16[4,256,1152]{2,1,0:T(8,128)(2,1)} %bitcast.210), calls=%async_computation | async-start | bytes 4718592 | tf_op jit(solution)/shard_map/all_to_all | solution.py:102
  137.8 7.9 %collective-permute-done.24 = bf16[128,1024]{1,0:T(8,128)(2,1)S(1)} collective-permute-done((bf16[128,1024]{1,0:T(8,128)(2,1)S(1)}, bf16[128,1024]{1,0:T(8,128)(2,1)S(1)}, u32[]{:S(2)}, u32[]{:S(2)}) %collective-permute-start.24) | collective-permute-done | bytes 262176 | tf_op jit(solution)/shard_map/ppermute | solution.py:26
  150.6 14.8 %all-to-all-done = bf16[4,256,1152]{2,1,0:T(8,128)(2,1)S(1)} async-done(((bf16[4,256,1152]{2,1,0:T(8,128)(2,1)}), bf16[4,256,1152]{2,1,0:T(8,128)(2,1)S(1)}, u32[]{:S(2)}, u32[]{:S(2)}) %all-to-all-start) | async-done | bytes 2359328 | tf_op jit(solution)/shard_map/all_to_all | solution.py:102
  173.7 2.4 multiply_reduce_fusion.3
  178.6 3.4 %collective-permute-done.29 = f32[2,256]{1,0:T(2,128)S(1)} collective-permute-done((f32[2,256]{1,0:T(2,128)S(1)}, f32[2,256]{1,0:T(2,128)S(1)}, u32[]{:S(2)}, u32[]{:S(2)}) %collective-permute-start.29) | collective-permute-done | bytes 2080 | tf_op jit(solution)/shard_map/ppermute | solution.py:149
  182.2 4.0 %multiply_reduce_fusion = (f32[1024]{0:T(1024)S(1)}, f32[512,1024]{1,0:T(8,128)}) fusion(bf16[128,1024]{1,0:T(8,128)(2,1)S(1)} %copy-done.22, bf16[128,1024]{1,0:T(8,128)(2,1)S(1)} %copy-done.24, bf16[128,1024]{1,0:T(8,128)(2,1)} %copy-done.25, bf16[128,1024]{1,0:T(8,128)(2,1)S(1)} %copy-done.20, bf16[1024,768]{1,0:T(8,128)(2,1)} %bitcast.214, ...), kind=kOutput, calls=%fused_computation.13 | convolution fusion | flops 812907520 | bytes 5509120 | tf_op jit(solution)/shard_map/dot_general | solution.py:15
  186.4 2.1 convolution_convert_fusion.2
  191.3 11.2 %all-to-all-start.1 = ((bf16[32,32,1152]{2,1,0:T(8,128)(2,1)}), bf16[32,32,1152]{2,1,0:T(8,128)(2,1)S(1)}, u32[]{:S(2)}, u32[]{:S(2)}) async-start(bf16[32,32,1152]{2,1,0:T(8,128)(2,1)} %pad_maximum_fusion), calls=%async_computation.1 | async-start | bytes 4718592 | tf_op jit(solution)/shard_map/all_to_all | solution.py:102
  212.9 2.1 collective-permute-start.36
  218.3 15.8 %collective-permute-done.34 = bf16[2,32,1152]{2,1,0:T(8,128)(2,1)S(1)} collective-permute-done((bf16[2,32,1152]{2,1,0:T(8,128)(2,1)S(1)}, bf16[2,32,1152]{2,1,0:T(8,128)(2,1)S(1)}, u32[]{:S(2)}, u32[]{:S(2)}) %collective-permute-start.34) | collective-permute-done | bytes 147488 | tf_op jit(solution)/shard_map/ppermute | solution.py:22
  234.8 4.0 %collective-permute-done.36 = bf16[2,32,1152]{2,1,0:T(8,128)(2,1)S(1)} collective-permute-done((bf16[2,32,1152]{2,1,0:T(8,128)(2,1)S(1)}, bf16[2,32,1152]{2,1,0:T(8,128)(2,1)S(1)}, u32[]{:S(2)}, u32[]{:S(2)}) %collective-permute-start.36) | collective-permute-done | bytes 147488 | tf_op jit(solution)/shard_map/ppermute | solution.py:22
  242.4 2.9 %reduce-scatter.5.cloned.1.call-done = bf16[64,2304]{1,0:T(8,128)(2,1)} async-done(((bf16[256,2304]{1,0:T(8,128)(2,1)}), bf16[64,2304]{1,0:T(8,128)(2,1)}) %reduce-scatter.5.cloned.1.call-update) | async-done | bytes 294928 | tf_op jit(solution)/shard_map/reduce_scatter | solution.py:230
  253.7 6.0 %collective-permute-done.37 = bf16[32,3456]{1,0:T(8,128)(2,1)S(1)} collective-permute-done((bf16[32,3456]{1,0:T(8,128)(2,1)S(1)}, bf16[32,3456]{1,0:T(8,128)(2,1)S(1)}, u32[]{:S(2)}, u32[]{:S(2)}) %collective-permute-start.37) | collective-permute-done | bytes 221216 | tf_op jit(solution)/shard_map/ppermute | solution.py:26
  (274 shorter events, 91.4 us)
Async XLA Ops:
  7.2 98.8 %all-gather.2.cloned.1.call-start = ((), (), s32[]{:S(2)}) async-start(), calls=%async_computation.4 | async-start | bytes 4866048 | tf_op jit(solution)/shard_map/all_gather | solution.py:176
  14.4 194.1 %reduce-scatter.3.cloned.1.call-start = ((), (), s32[]{:S(2)}) async-start(), calls=%async_computation.5 | async-start | bytes 5898240 | tf_op jit(solution)/shard_map/reduce_scatter | solution.py:229
  18.2 10.9 %collective-permute-start.3 = (bf16[2,32,768]{2,1,0:T(8,128)(2,1)S(1)}, bf16[2,32,768]{2,1,0:T(8,128)(2,1)S(1)}, u32[]{:S(2)}, u32[]{:S(2)}) collective-permute-start(bf16[2,32,768]{2,1,0:T(8,128)(2,1)S(1)} %get-tuple-element.48), channel_id=1, source_target_pairs={{0,16},{16,32},{32,48},{48,0},{1,17},{17,33},{33,49},{49,1},{2,18}... | collective-permute-start | bytes 294920 | tf_op jit(solution)/shard_map/ppermute | solution.py:22
  20.2 10.8 %collective-permute-start.4 = (bf16[2,32,768]{2,1,0:T(8,128)(2,1)S(1)}, bf16[2,32,768]{2,1,0:T(8,128)(2,1)S(1)}, u32[]{:S(2)}, u32[]{:S(2)}) collective-permute-start(bf16[2,32,768]{2,1,0:T(8,128)(2,1)S(1)} %get-tuple-element.48), channel_id=1, source_target_pairs={{0,48},{16,0},{32,16},{48,32},{1,49},{17,1},{33,17},{49,33},{2,50}... | collective-permute-start | bytes 294920 | tf_op jit(solution)/shard_map/ppermute | solution.py:22
  22.4 10.3 %collective-permute-start.5 = (bf16[2,32,768]{2,1,0:T(8,128)(2,1)S(1)}, bf16[2,32,768]{2,1,0:T(8,128)(2,1)S(1)}, u32[]{:S(2)}, u32[]{:S(2)}) collective-permute-start(bf16[2,32,768]{2,1,0:T(8,128)(2,1)S(1)} %get-tuple-element.48), channel_id=1, source_target_pairs={{0,32},{16,48},{32,0},{48,16},{1,33},{17,49},{33,1},{49,17},{2,34}... | collective-permute-start | bytes 294920 | tf_op jit(solution)/shard_map/ppermute | solution.py:22
  24.8 8.8 %collective-permute-start.10 = (bf16[2,32,1408]{2,1,0:T(8,128)(2,1)S(1)}, bf16[2,32,1408]{2,1,0:T(8,128)(2,1)S(1)}, u32[]{:S(2)}, u32[]{:S(2)}) collective-permute-start(bf16[2,32,1408]{2,1,0:T(8,128)(2,1)S(1)} %get-tuple-element.50), channel_id=1, source_target_pairs={{0,4},{4,8},{8,12},{12,0},{1,5},{5,9},{9,13},{13,1},{2,6},{6,10},{... | collective-permute-start | bytes 540680 | tf_op jit(solution)/shard_map/ppermute | solution.py:22
  26.4 10.0 %collective-permute-start.11 = (bf16[2,32,1408]{2,1,0:T(8,128)(2,1)S(1)}, bf16[2,32,1408]{2,1,0:T(8,128)(2,1)S(1)}, u32[]{:S(2)}, u32[]{:S(2)}) collective-permute-start(bf16[2,32,1408]{2,1,0:T(8,128)(2,1)S(1)} %get-tuple-element.50), channel_id=1, source_target_pairs={{0,12},{4,0},{8,4},{12,8},{1,13},{5,1},{9,5},{13,9},{2,14},{6,2},{... | collective-permute-start | bytes 540680 | tf_op jit(solution)/shard_map/ppermute | solution.py:22
  29.1 9.7 %collective-permute-start.12 = (bf16[2,32,1408]{2,1,0:T(8,128)(2,1)S(1)}, bf16[2,32,1408]{2,1,0:T(8,128)(2,1)S(1)}, u32[]{:S(2)}, u32[]{:S(2)}) collective-permute-start(bf16[2,32,1408]{2,1,0:T(8,128)(2,1)S(1)} %get-tuple-element.50), channel_id=1, source_target_pairs={{0,8},{4,12},{8,0},{12,4},{1,9},{5,13},{9,1},{13,5},{2,10},{6,14},... | collective-permute-start | bytes 540680 | tf_op jit(solution)/shard_map/ppermute | solution.py:22
  31.0 9.0 %collective-permute-start.1 = (bf16[128,1024]{1,0:T(8,128)(2,1)S(1)}, bf16[128,1024]{1,0:T(8,128)(2,1)S(1)}, u32[]{:S(2)}, u32[]{:S(2)}) collective-permute-start(bf16[128,1024]{1,0:T(8,128)(2,1)S(1)} %fusion.20), channel_id=1, source_target_pairs={{0,2},{2,0},{1,3},{3,1},{4,6},{6,4},{5,7},{7,5},{8,10},{10,8},{9,1... | collective-permute-start | bytes 786440 | tf_op jit(solution)/shard_map/ppermute | solution.py:26
  32.7 14.1 %collective-permute-start.6 = (bf16[2,4,32,768]{3,2,1,0:T(8,128)(2,1)S(1)}, bf16[2,4,32,768]{3,2,1,0:T(8,128)(2,1)S(1)}, u32[]{:S(2)}, u32[]{:S(2)}) collective-permute-start(bf16[2,4,32,768]{3,2,1,0:T(8,128)(2,1)S(1)} %bitcast_dynamic-update-slice_fusion.14), channel_id=1, source_target_pairs={{0,4},{4,8},{8,12},{12,0},{1,5},{5,9},{9,13},{13,1},{2,6},{6,10},{... | collective-permute-start | bytes 1179656 | tf_op jit(solution)/shard_map/ppermute | solution.py:22
  33.6 14.6 %collective-permute-start.7 = (bf16[2,4,32,768]{3,2,1,0:T(8,128)(2,1)S(1)}, bf16[2,4,32,768]{3,2,1,0:T(8,128)(2,1)S(1)}, u32[]{:S(2)}, u32[]{:S(2)}) collective-permute-start(bf16[2,4,32,768]{3,2,1,0:T(8,128)(2,1)S(1)} %bitcast_dynamic-update-slice_fusion.14), channel_id=1, source_target_pairs={{0,12},{4,0},{8,4},{12,8},{1,13},{5,1},{9,5},{13,9},{2,14},{6,2},{... | collective-permute-start | bytes 1179656 | tf_op jit(solution)/shard_map/ppermute | solution.py:22
  36.3 21.0 %collective-permute-start.8 = (bf16[2,4,32,768]{3,2,1,0:T(8,128)(2,1)S(1)}, bf16[2,4,32,768]{3,2,1,0:T(8,128)(2,1)S(1)}, u32[]{:S(2)}, u32[]{:S(2)}) collective-permute-start(bf16[2,4,32,768]{3,2,1,0:T(8,128)(2,1)S(1)} %bitcast_dynamic-update-slice_fusion.14), channel_id=1, source_target_pairs={{0,8},{4,12},{8,0},{12,4},{1,9},{5,13},{9,1},{13,5},{2,10},{6,14},... | collective-permute-start | bytes 1179656 | tf_op jit(solution)/shard_map/ppermute | solution.py:22
  38.8 27.2 %collective-permute-start.13 = (bf16[2,4,32,1408]{3,2,1,0:T(8,128)(2,1)S(1)}, bf16[2,4,32,1408]{3,2,1,0:T(8,128)(2,1)S(1)}, u32[]{:S(2)}, u32[]{:S(2)}) collective-permute-start(bf16[2,4,32,1408]{3,2,1,0:T(8,128)(2,1)S(1)} %bitcast_dynamic-update-slice_fusion.7), channel_id=1, source_target_pairs={{0,16},{16,32},{32,48},{48,0},{1,17},{17,33},{33,49},{49,1},{2,18}... | collective-permute-start | bytes 2162696 | tf_op jit(solution)/shard_map/ppermute | solution.py:22
  40.0 29.4 %collective-permute-start.14 = (bf16[2,4,32,1408]{3,2,1,0:T(8,128)(2,1)S(1)}, bf16[2,4,32,1408]{3,2,1,0:T(8,128)(2,1)S(1)}, u32[]{:S(2)}, u32[]{:S(2)}) collective-permute-start(bf16[2,4,32,1408]{3,2,1,0:T(8,128)(2,1)S(1)} %bitcast_dynamic-update-slice_fusion.7), channel_id=1, source_target_pairs={{0,48},{16,0},{32,16},{48,32},{1,49},{17,1},{33,17},{49,33},{2,50}... | collective-permute-start | bytes 2162696 | tf_op jit(solution)/shard_map/ppermute | solution.py:22
  46.8 10.6 %collective-permute-start.2 = (bf16[256,1024]{1,0:T(8,128)(2,1)S(1)}, bf16[256,1024]{1,0:T(8,128)(2,1)S(1)}, u32[]{:S(2)}, u32[]{:S(2)}) collective-permute-start(bf16[256,1024]{1,0:T(8,128)(2,1)S(1)} %pad_maximum_fusion.9), channel_id=1, source_target_pairs={{0,1},{1,0},{2,3},{3,2},{4,5},{5,4},{6,7},{7,6},{8,9},{9,8},{10,11... | collective-permute-start | bytes 1572872 | tf_op jit(solution)/shard_map/ppermute | solution.py:26
  66.0 14.8 %collective-permute-start.15 = (bf16[1,4,32,1408]{3,2,1,0:T(8,128)(2,1)S(1)}, bf16[1,4,32,1408]{3,2,1,0:T(8,128)(2,1)S(1)}, u32[]{:S(2)}, u32[]{:S(2)}) collective-permute-start(bf16[1,4,32,1408]{3,2,1,0:T(8,128)(2,1)S(1)} %slice.288), channel_id=1, source_target_pairs={{0,16},{16,32},{32,48},{48,0},{1,17},{17,33},{33,49},{49,1},{2,18}... | collective-permute-start | bytes 1081352 | tf_op jit(solution)/shard_map/ppermute | solution.py:22
  69.4 13.7 %collective-permute-start.16 = (bf16[1,4,32,1408]{3,2,1,0:T(8,128)(2,1)S(1)}, bf16[1,4,32,1408]{3,2,1,0:T(8,128)(2,1)S(1)}, u32[]{:S(2)}, u32[]{:S(2)}) collective-permute-start(bf16[1,4,32,1408]{3,2,1,0:T(8,128)(2,1)S(1)} %slice.289), channel_id=1, source_target_pairs={{0,48},{16,0},{32,16},{48,32},{1,49},{17,1},{33,17},{49,33},{2,50}... | collective-permute-start | bytes 1081352 | tf_op jit(solution)/shard_map/ppermute | solution.py:22
  86.0 9.2 %collective-permute-start.18 = (bf16[128,1024]{1,0:T(8,128)(2,1)S(1)}, bf16[128,1024]{1,0:T(8,128)(2,1)S(1)}, u32[]{:S(2)}, u32[]{:S(2)}) collective-permute-start(bf16[128,1024]{1,0:T(8,128)(2,1)S(1)} %slice.425), channel_id=1, source_target_pairs={{0,2},{2,0},{1,3},{3,1},{4,6},{6,4},{5,7},{7,5},{8,10},{10,8},{9,1... | collective-permute-start | bytes 786440 | tf_op jit(solution)/shard_map/ppermute | solution.py:26
  87.2 13.7 %collective-permute-start.21 = (bf16[128,1024]{0,1:T(8,128)(2,1)S(1)}, bf16[128,1024]{0,1:T(8,128)(2,1)S(1)}, u32[]{:S(2)}, u32[]{:S(2)}) collective-permute-start(bf16[128,1024]{0,1:T(8,128)(2,1)S(1)} %copy.38), channel_id=1, source_target_pairs={{0,2},{2,0},{1,3},{3,1},{4,6},{6,4},{5,7},{7,5},{8,10},{10,8},{9,1... | collective-permute-start | bytes 786440 | tf_op jit(solution)/shard_map/ppermute | solution.py:26
  95.6 10.4 %collective-permute-start.19 = (bf16[128,1024]{1,0:T(8,128)(2,1)S(1)}, bf16[128,1024]{1,0:T(8,128)(2,1)S(1)}, u32[]{:S(2)}, u32[]{:S(2)}) collective-permute-start(bf16[128,1024]{1,0:T(8,128)(2,1)S(1)} %multiply_convert_fusion.4), channel_id=1, source_target_pairs={{0,2},{2,0},{1,3},{3,1},{4,6},{6,4},{5,7},{7,5},{8,10},{10,8},{9,1... | collective-permute-start | bytes 786440 | tf_op jit(solution)/shard_map/ppermute | solution.py:26
  131.2 34.2 %all-to-all-start = ((bf16[4,256,1152]{2,1,0:T(8,128)(2,1)}), bf16[4,256,1152]{2,1,0:T(8,128)(2,1)S(1)}, u32[]{:S(2)}, u32[]{:S(2)}) async-start(bf16[4,256,1152]{2,1,0:T(8,128)(2,1)} %bitcast.210), calls=%async_computation | async-start | bytes 4718592 | tf_op jit(solution)/shard_map/all_to_all | solution.py:102
  146.9 21.6 %collective-permute-start.25 = (bf16[128,1024]{1,0:T(8,128)(2,1)S(1)}, bf16[128,1024]{1,0:T(8,128)(2,1)}, u32[]{:S(2)}, u32[]{:S(2)}) collective-permute-start(bf16[128,1024]{1,0:T(8,128)(2,1)S(1)} %get-tuple-element.39), channel_id=1, source_target_pairs={{0,2},{2,0},{1,3},{3,1},{4,6},{6,4},{5,7},{7,5},{8,10},{10,8},{9,1... | collective-permute-start | bytes 786440 | tf_op jit(solution)/shard_map/ppermute | solution.py:26
  150.6 19.2 %collective-permute-start.27 = (bf16[256,1024]{1,0:T(8,128)(2,1)}, bf16[256,1024]{1,0:T(8,128)(2,1)}, u32[]{:S(2)}, u32[]{:S(2)}) collective-permute-start(bf16[256,1024]{1,0:T(8,128)(2,1)} %slice.419), channel_id=1, source_target_pairs={{0,1},{1,0},{2,3},{3,2},{4,5},{5,4},{6,7},{7,6},{8,9},{9,8},{10,11... | collective-permute-start | bytes 1572872 | tf_op jit(solution)/shard_map/ppermute | solution.py:26
  172.2 32.7 %collective-permute-start.28 = (bf16[128,1024]{1,0:T(8,128)(2,1)}, bf16[128,1024]{1,0:T(8,128)(2,1)}, u32[]{:S(2)}, u32[]{:S(2)}) collective-permute-start(bf16[128,1024]{1,0:T(8,128)(2,1)} %slice.423), channel_id=1, source_target_pairs={{0,2},{2,0},{1,3},{3,1},{4,6},{6,4},{5,7},{7,5},{8,10},{10,8},{9,1... | collective-permute-start | bytes 786440 | tf_op jit(solution)/shard_map/ppermute | solution.py:26
  191.3 49.7 %all-to-all-start.1 = ((bf16[32,32,1152]{2,1,0:T(8,128)(2,1)}), bf16[32,32,1152]{2,1,0:T(8,128)(2,1)S(1)}, u32[]{:S(2)}, u32[]{:S(2)}) async-start(bf16[32,32,1152]{2,1,0:T(8,128)(2,1)} %pad_maximum_fusion), calls=%async_computation.1 | async-start | bytes 4718592 | tf_op jit(solution)/shard_map/all_to_all | solution.py:102
  202.6 42.7 %reduce-scatter.5.cloned.1.call-start = ((), (), s32[]{:S(2)}) async-start(), calls=%async_computation.6 | async-start | bytes 1474560 | tf_op jit(solution)/shard_map/reduce_scatter | solution.py:230
  204.9 11.4 %collective-permute-start.30 = (bf16[256,1024]{1,0:T(8,128)(2,1)}, bf16[256,1024]{1,0:T(8,128)(2,1)}, u32[]{:S(2)}, u32[]{:S(2)}) collective-permute-start(bf16[256,1024]{1,0:T(8,128)(2,1)} %pad_maximum_fusion.13), channel_id=1, source_target_pairs={{0,1},{1,0},{2,3},{3,2},{4,5},{5,4},{6,7},{7,6},{8,9},{9,8},{10,11... | collective-permute-start | bytes 1572872 | tf_op jit(solution)/shard_map/ppermute | solution.py:26
  209.6 24.5 %collective-permute-start.34 = (bf16[2,32,1152]{2,1,0:T(8,128)(2,1)S(1)}, bf16[2,32,1152]{2,1,0:T(8,128)(2,1)S(1)}, u32[]{:S(2)}, u32[]{:S(2)}) collective-permute-start(bf16[2,32,1152]{2,1,0:T(8,128)(2,1)S(1)} %get-tuple-element.68), channel_id=1, source_target_pairs={{0,4},{4,8},{8,12},{12,0},{1,5},{5,9},{9,13},{13,1},{2,6},{6,10},{... | collective-permute-start | bytes 442376 | tf_op jit(solution)/shard_map/ppermute | solution.py:22
  211.5 23.3 %collective-permute-start.35 = (bf16[2,32,1152]{2,1,0:T(8,128)(2,1)S(1)}, bf16[2,32,1152]{2,1,0:T(8,128)(2,1)S(1)}, u32[]{:S(2)}, u32[]{:S(2)}) collective-permute-start(bf16[2,32,1152]{2,1,0:T(8,128)(2,1)S(1)} %get-tuple-element.69), channel_id=1, source_target_pairs={{0,12},{4,0},{8,4},{12,8},{1,13},{5,1},{9,5},{13,9},{2,14},{6,2},{... | collective-permute-start | bytes 442376 | tf_op jit(solution)/shard_map/ppermute | solution.py:22
  212.9 25.8 %collective-permute-start.36 = (bf16[2,32,1152]{2,1,0:T(8,128)(2,1)S(1)}, bf16[2,32,1152]{2,1,0:T(8,128)(2,1)S(1)}, u32[]{:S(2)}, u32[]{:S(2)}) collective-permute-start(bf16[2,32,1152]{2,1,0:T(8,128)(2,1)S(1)} %get-tuple-element.70), channel_id=1, source_target_pairs={{0,8},{4,12},{8,0},{12,4},{1,9},{5,13},{9,1},{13,5},{2,10},{6,14},... | collective-permute-start | bytes 442376 | tf_op jit(solution)/shard_map/ppermute | solution.py:22
  217.6 22.1 %collective-permute-start.31 = (bf16[128,1024]{1,0:T(8,128)(2,1)S(1)}, bf16[128,1024]{1,0:T(8,128)(2,1)S(1)}, u32[]{:S(2)}, u32[]{:S(2)}) collective-permute-start(bf16[128,1024]{1,0:T(8,128)(2,1)S(1)} %slice.422), channel_id=1, source_target_pairs={{0,2},{2,0},{1,3},{3,1},{4,6},{6,4},{5,7},{7,5},{8,10},{10,8},{9,1... | collective-permute-start | bytes 786440 | tf_op jit(solution)/shard_map/ppermute | solution.py:26
  251.0 8.8 %collective-permute-start.37 = (bf16[32,3456]{1,0:T(8,128)(2,1)S(1)}, bf16[32,3456]{1,0:T(8,128)(2,1)S(1)}, u32[]{:S(2)}, u32[]{:S(2)}) collective-permute-start(bf16[32,3456]{1,0:T(8,128)(2,1)S(1)} %fusion.47), channel_id=1, source_target_pairs={{0,64},{64,0},{1,65},{65,1},{2,66},{66,2},{3,67},{67,3},{4,68},{68... | collective-permute-start | bytes 663560 | tf_op jit(solution)/shard_map/ppermute | solution.py:26
  (49 other events, 219.7 us)
Sparse Core Ops, SparseCore 0:
  14.5 85.0 all-gather.1
  129.2 53.2 reduce-scatter.2
  208.6 36.6 reduce-scatter.4

commit v2 on v1

--- a/solution.py
+++ b/solution.py
@@ -232,7 +232,7 @@
     gain_two_grad = jnp.sum(grad_normed_two * normed_two, axis=0)
     grad_middle = cotangent.astype(F32) + norm_back(grad_normed_two, gain_two, scale_two, normed_two)
     grad_mid_low = grad_middle.astype(BF16)
-    grad_mid_far = no_sooner(swapped(grad_mid_low, "yl"), down_part)
+    grad_mid_far = after(swapped(grad_mid_low, "yl"), down_part)
     grad_mix_rows = reordered(gather_core(grad_mid_low, grad_mid_far))
     ffn_terms = dot(after(hidden, grad_mid_low), down_full, 1, 1)
     mixed = (middle + scatter_tokens(after(ffn_terms, grad_mix_rows))).astype(BF16)
@@ -288,7 +288,7 @@
     sums = jnp.concatenate(
         [sums[:, :per].reshape(1, width), sums[:, per : 2 * per].reshape(1, width), conv_sum]
     )
-    sums = no_sooner(sums, gate_part)
+    sums = after(sums, gate_part)
     sums = sums + swapped(sums, "core")
     sums = sums + swapped(sums, "yl")
 

time: 270 us -> 267 us (0.989)
  local copies, waits for them, and re-layouts: 25.1 us -> 21.5 us
    unnamed x80 -> x82, local copies, waits for them, and re-layouts: 8 us -> 7.31 us
  transfers between devices with their start and end apart: 43 -> 43, of which waited for: 22 -> 21; matrix products, arithmetic and copies ran while one was open for 19% -> 19% of each run, Pallas kernels for 0% -> 0%
where the time goes in v2:
time: 267 us; the launch traced here: 266 us
  waiting for transfers between devices  107 us (40%)
  starting transfers between devices  62 us (23%)
  matrix products  30.4 us (11%)
  other arithmetic  28.1 us (11%)
  local copies, waits for them, and re-layouts  21.5 us (8%)
  between operations  16.3 us (6%)
    ppermute x16, waiting for transfers between devices, shifted(): lax.ppermute(value, axis, [(i, (i + by) % size) for i in range(size)])  49.3 us
    ppermute x20, waiting for transfers between devices, swapped(): return lax.ppermute(value, axis, [(0, 1), (1, 0)])  33.9 us
    dot_general x14, matrix products, dot(): lax.dot_general(lhs, rhs, (((lhs_dim,), (rhs_dim,)), ((), ())), preferred...  30.4 us
    ppermute x16, starting transfers between devices, shifted(): lax.ppermute(value, axis, [(i, (i + by) % size) for i in range(size)])  27.6 us
    all_to_all x2, starting transfers between devices, exchange_sum(): parts = lax.all_to_all(whole.reshape(count, -1, whole.shape[1]), axes, 0, 0)  16.6 us
    all_to_all x2, waiting for transfers between devices, exchange_sum(): parts = lax.all_to_all(whole.reshape(count, -1, whole.shape[1]), axes, 0, 0)  14.8 us
    ppermute x20, starting transfers between devices, swapped(): return lax.ppermute(value, axis, [(0, 1), (1, 0)])  12.7 us
    unnamed x82, local copies, waits for them, and re-layouts  7.31 us
  transfers between devices with their start and end apart: 43, of which 21 were waited for; matrix products, arithmetic and copies ran while one was open for 19% of the time, Pallas kernels for 0%

profile of v2, /device:TPU:0, one launch (start us, length us, event | category | flops | bytes accessed | tf_op | source)
XLA Modules:
  0.0 265.5 jit_solution(5066149630743247959)
XLA Ops:
  11.0 3.3 %collective-permute-start = (bf16[32,2176]{1,0:T(8,128)(2,1)S(1)}, bf16[32,2176]{1,0:T(8,128)(2,1)S(1)}, u32[]{:S(2)}, u32[]{:S(2)}) collective-permute-start(bf16[32,2176]{1,0:T(8,128)(2,1)S(1)} %bitcast_dynamic-update-slice_fusion.15), channel_id=1, source_target_pairs={{0,64},{64,0},{1,65},{65,1},{2,66},{66,2},{3,67},{67,3},{4,68},{68... | collective-permute-start | bytes 417800 | tf_op jit(solution)/shard_map/ppermute | solution.py:26
  20.2 2.2 collective-permute-start.4
  33.6 2.7 %collective-permute-start.7 = (bf16[2,4,32,768]{3,2,1,0:T(8,128)(2,1)S(1)}, bf16[2,4,32,768]{3,2,1,0:T(8,128)(2,1)S(1)}, u32[]{:S(2)}, u32[]{:S(2)}) collective-permute-start(bf16[2,4,32,768]{3,2,1,0:T(8,128)(2,1)S(1)} %bitcast_dynamic-update-slice_fusion.14), channel_id=1, source_target_pairs={{0,12},{4,0},{8,4},{12,8},{1,13},{5,1},{9,5},{13,9},{2,14},{6,2},{... | collective-permute-start | bytes 1179656 | tf_op jit(solution)/shard_map/ppermute | solution.py:22
  40.0 2.1 collective-permute-start.14
  42.2 4.6 %collective-permute-done.6 = bf16[2,4,32,768]{3,2,1,0:T(8,128)(2,1)S(1)} collective-permute-done((bf16[2,4,32,768]{3,2,1,0:T(8,128)(2,1)S(1)}, bf16[2,4,32,768]{3,2,1,0:T(8,128)(2,1)S(1)}, u32[]{:S(2)}, u32[]{:S(2)}) %collective-permute-start.6) | collective-permute-done | bytes 393248 | tf_op jit(solution)/shard_map/ppermute | solution.py:22
  48.3 9.1 %collective-permute-done.8 = bf16[2,4,32,768]{3,2,1,0:T(8,128)(2,1)S(1)} collective-permute-done((bf16[2,4,32,768]{3,2,1,0:T(8,128)(2,1)S(1)}, bf16[2,4,32,768]{3,2,1,0:T(8,128)(2,1)S(1)}, u32[]{:S(2)}, u32[]{:S(2)}) %collective-permute-start.8) | collective-permute-done | bytes 393248 | tf_op jit(solution)/shard_map/ppermute | solution.py:22
  59.8 3.6 %collective-permute-start.9 = (f32[3,256]{1,0:T(4,128)S(1)}, f32[3,256]{1,0:T(4,128)S(1)}, u32[]{:S(2)}, u32[]{:S(2)}) collective-permute-start(f32[3,256]{1,0:T(4,128)S(1)} %select_maximum_fusion), channel_id=1, source_target_pairs={{0,4},{4,8},{8,12},{12,16},{16,20},{20,24},{24,28},{28,32},{32,36}... | collective-permute-start | bytes 9224 | tf_op jit(solution)/shard_map/ppermute | solution.py:149
  66.1 3.4 %collective-permute-start.15 = (bf16[1,4,32,1408]{3,2,1,0:T(8,128)(2,1)S(1)}, bf16[1,4,32,1408]{3,2,1,0:T(8,128)(2,1)S(1)}, u32[]{:S(2)}, u32[]{:S(2)}) collective-permute-start(bf16[1,4,32,1408]{3,2,1,0:T(8,128)(2,1)S(1)} %slice.280), channel_id=1, source_target_pairs={{0,16},{16,32},{32,48},{48,0},{1,17},{17,33},{33,49},{49,1},{2,18}... | collective-permute-start | bytes 1081352 | tf_op jit(solution)/shard_map/ppermute | solution.py:22
  69.8 11.1 %collective-permute-done.15 = bf16[1,4,32,1408]{3,2,1,0:T(8,128)(2,1)S(1)} collective-permute-done((bf16[1,4,32,1408]{3,2,1,0:T(8,128)(2,1)S(1)}, bf16[1,4,32,1408]{3,2,1,0:T(8,128)(2,1)S(1)}, u32[]{:S(2)}, u32[]{:S(2)}) %collective-permute-start.15) | collective-permute-done | bytes 360480 | tf_op jit(solution)/shard_map/ppermute | solution.py:22
  80.9 2.3 collective-permute-done.16
  88.6 6.9 %collective-permute-done.18 = bf16[128,1024]{1,0:T(8,128)(2,1)S(1)} collective-permute-done((bf16[128,1024]{1,0:T(8,128)(2,1)S(1)}, bf16[128,1024]{1,0:T(8,128)(2,1)S(1)}, u32[]{:S(2)}, u32[]{:S(2)}) %collective-permute-start.18) | collective-permute-done | bytes 262176 | tf_op jit(solution)/shard_map/ppermute | solution.py:26
  96.6 4.4 %collective-permute-done.21 = bf16[128,1024]{0,1:T(8,128)(2,1)S(1)} collective-permute-done((bf16[128,1024]{0,1:T(8,128)(2,1)S(1)}, bf16[128,1024]{0,1:T(8,128)(2,1)S(1)}, u32[]{:S(2)}, u32[]{:S(2)}) %collective-permute-start.21) | collective-permute-done | bytes 262176 | tf_op jit(solution)/shard_map/ppermute | solution.py:26
  101.2 4.8 %collective-permute-done.19 = bf16[128,1024]{1,0:T(8,128)(2,1)S(1)} collective-permute-done((bf16[128,1024]{1,0:T(8,128)(2,1)S(1)}, bf16[128,1024]{1,0:T(8,128)(2,1)S(1)}, u32[]{:S(2)}, u32[]{:S(2)}) %collective-permute-start.19) | collective-permute-done | bytes 262176 | tf_op jit(solution)/shard_map/ppermute | solution.py:26
  111.7 2.4 multiply_convert_fusion
  114.2 2.9 %convolution_convert_fusion.1 = bf16[1024,1152]{1,0:T(8,128)(2,1)} fusion(bf16[512,1024]{0,1:T(8,128)(2,1)S(1)} %bitcast.218, bf16[512,1152]{1,0:T(8,128)(2,1)S(1)} %get-tuple-element.32), kind=kOutput, calls=%fused_computation.2 | convolution fusion | flops 1209139200 | bytes 4587520 | tf_op jit(solution)/shard_map/dot_general | solution.py:15
  118.7 2.9 %fusion.11 = f32[512,1024]{1,0:T(8,128)} fusion(f32[512,1024]{1,0:T(8,128)S(1)} %fusion.3, bf16[512,1152]{1,0:T(8,128)(2,1)S(1)} %get-tuple-element.55, bf16[2,1024,1152]{2,1,0:T(8,128)(2,1)S(1)} %copy-done.32), kind=kOutput, calls=%fused_computation.23 | convolution fusion | flops 1208483840 | bytes 7733248 | tf_op jit(solution)/shard_map/dot_general | solution.py:15
  123.4 5.6 %convolution_convert_fusion = bf16[1024,2304]{1,0:T(8,128)(2,1)} fusion(bf16[512,1024]{0,1:T(8,128)(2,1)S(1)} %bitcast.219, bf16[512,1152]{1,0:T(8,128)(2,1)S(1)} %copy-done.34, bf16[512,1152]{1,0:T(8,128)(2,1)} %copy-done.37), kind=kOutput, calls=%fused_computation | convolution fusion | flops 2422996992 | bytes 8126464 | tf_op jit(solution)/shard_map/dot_general | solution.py:15
  129.0 2.1 slice.410
  131.2 4.4 %all-to-all-start = ((bf16[4,256,1152]{2,1,0:T(8,128)(2,1)}), bf16[4,256,1152]{2,1,0:T(8,128)(2,1)S(1)}, u32[]{:S(2)}, u32[]{:S(2)}) async-start(bf16[4,256,1152]{2,1,0:T(8,128)(2,1)} %bitcast.207), calls=%async_computation | async-start | bytes 4718592 | tf_op jit(solution)/shard_map/all_to_all | solution.py:102
  137.8 7.9 %collective-permute-done.24 = bf16[128,1024]{1,0:T(8,128)(2,1)S(1)} collective-permute-done((bf16[128,1024]{1,0:T(8,128)(2,1)S(1)}, bf16[128,1024]{1,0:T(8,128)(2,1)S(1)}, u32[]{:S(2)}, u32[]{:S(2)}) %collective-permute-start.24) | collective-permute-done | bytes 262176 | tf_op jit(solution)/shard_map/ppermute | solution.py:26
  150.5 14.8 %all-to-all-done = bf16[4,256,1152]{2,1,0:T(8,128)(2,1)S(1)} async-done(((bf16[4,256,1152]{2,1,0:T(8,128)(2,1)}), bf16[4,256,1152]{2,1,0:T(8,128)(2,1)S(1)}, u32[]{:S(2)}, u32[]{:S(2)}) %all-to-all-start) | async-done | bytes 2359328 | tf_op jit(solution)/shard_map/all_to_all | solution.py:102
  172.1 2.4 multiply_reduce_fusion.3
  177.0 3.4 %collective-permute-done.29 = f32[2,256]{1,0:T(2,128)S(1)} collective-permute-done((f32[2,256]{1,0:T(2,128)S(1)}, f32[2,256]{1,0:T(2,128)S(1)}, u32[]{:S(2)}, u32[]{:S(2)}) %collective-permute-start.29) | collective-permute-done | bytes 2080 | tf_op jit(solution)/shard_map/ppermute | solution.py:149
  180.6 4.1 %multiply_reduce_fusion = (f32[1024]{0:T(1024)S(1)}, f32[512,1024]{1,0:T(8,128)}) fusion(bf16[128,1024]{1,0:T(8,128)(2,1)S(1)} %copy-done.23, bf16[128,1024]{1,0:T(8,128)(2,1)S(1)} %copy-done.25, bf16[128,1024]{1,0:T(8,128)(2,1)} %copy-done.26, bf16[128,1024]{1,0:T(8,128)(2,1)S(1)} %copy-done.21, bf16[1024,768]{1,0:T(8,128)(2,1)} %bitcast.212, ...), kind=kOutput, calls=%fused_computation.13 | convolution fusion | flops 812907520 | bytes 5509120 | tf_op jit(solution)/shard_map/dot_general | solution.py:15
  184.9 2.1 convolution_convert_fusion.2
  189.7 12.2 %all-to-all-start.1 = ((bf16[32,32,1152]{2,1,0:T(8,128)(2,1)}), bf16[32,32,1152]{2,1,0:T(8,128)(2,1)S(1)}, u32[]{:S(2)}, u32[]{:S(2)}) async-start(bf16[32,32,1152]{2,1,0:T(8,128)(2,1)} %pad_maximum_fusion), calls=%async_computation.1 | async-start | bytes 4718592 | tf_op jit(solution)/shard_map/all_to_all | solution.py:102
  213.9 2.2 collective-permute-start.36
  217.7 16.7 %collective-permute-done.34 = bf16[2,32,1152]{2,1,0:T(8,128)(2,1)S(1)} collective-permute-done((bf16[2,32,1152]{2,1,0:T(8,128)(2,1)}, bf16[2,32,1152]{2,1,0:T(8,128)(2,1)S(1)}, u32[]{:S(2)}, u32[]{:S(2)}) %collective-permute-start.34) | collective-permute-done | bytes 147488 | tf_op jit(solution)/shard_map/ppermute | solution.py:22
  234.4 2.4 collective-permute-done.36
  240.5 4.8 %reduce-scatter.5.cloned.1.call-done = bf16[64,2304]{1,0:T(8,128)(2,1)} async-done(((bf16[256,2304]{1,0:T(8,128)(2,1)}), bf16[64,2304]{1,0:T(8,128)(2,1)}) %reduce-scatter.5.cloned.1.call-update) | async-done | bytes 294928 | tf_op jit(solution)/shard_map/reduce_scatter | solution.py:230
  247.6 2.1 collective-permute-start.37
  251.7 4.9 %collective-permute-done.37 = bf16[32,3456]{1,0:T(8,128)(2,1)S(1)} collective-permute-done((bf16[32,3456]{1,0:T(8,128)(2,1)S(1)}, bf16[32,3456]{1,0:T(8,128)(2,1)S(1)}, u32[]{:S(2)}, u32[]{:S(2)}) %collective-permute-start.37) | collective-permute-done | bytes 221216 | tf_op jit(solution)/shard_map/ppermute | solution.py:26
  (274 shorter events, 88.4 us)
Async XLA Ops:
  7.2 98.8 %all-gather.2.cloned.1.call-start = ((), (), s32[]{:S(2)}) async-start(), calls=%async_computation.4 | async-start | bytes 4866048 | tf_op jit(solution)/shard_map/all_gather | solution.py:176
  14.4 198.5 %reduce-scatter.3.cloned.1.call-start = ((), (), s32[]{:S(2)}) async-start(), calls=%async_computation.5 | async-start | bytes 5898240 | tf_op jit(solution)/shard_map/reduce_scatter | solution.py:229
  18.2 10.9 %collective-permute-start.3 = (bf16[2,32,768]{2,1,0:T(8,128)(2,1)S(1)}, bf16[2,32,768]{2,1,0:T(8,128)(2,1)S(1)}, u32[]{:S(2)}, u32[]{:S(2)}) collective-permute-start(bf16[2,32,768]{2,1,0:T(8,128)(2,1)S(1)} %get-tuple-element.52), channel_id=1, source_target_pairs={{0,16},{16,32},{32,48},{48,0},{1,17},{17,33},{33,49},{49,1},{2,18}... | collective-permute-start | bytes 294920 | tf_op jit(solution)/shard_map/ppermute | solution.py:22
  20.2 10.8 %collective-permute-start.4 = (bf16[2,32,768]{2,1,0:T(8,128)(2,1)S(1)}, bf16[2,32,768]{2,1,0:T(8,128)(2,1)S(1)}, u32[]{:S(2)}, u32[]{:S(2)}) collective-permute-start(bf16[2,32,768]{2,1,0:T(8,128)(2,1)S(1)} %get-tuple-element.52), channel_id=1, source_target_pairs={{0,48},{16,0},{32,16},{48,32},{1,49},{17,1},{33,17},{49,33},{2,50}... | collective-permute-start | bytes 294920 | tf_op jit(solution)/shard_map/ppermute | solution.py:22
  22.4 10.3 %collective-permute-start.5 = (bf16[2,32,768]{2,1,0:T(8,128)(2,1)S(1)}, bf16[2,32,768]{2,1,0:T(8,128)(2,1)S(1)}, u32[]{:S(2)}, u32[]{:S(2)}) collective-permute-start(bf16[2,32,768]{2,1,0:T(8,128)(2,1)S(1)} %get-tuple-element.52), channel_id=1, source_target_pairs={{0,32},{16,48},{32,0},{48,16},{1,33},{17,49},{33,1},{49,17},{2,34}... | collective-permute-start | bytes 294920 | tf_op jit(solution)/shard_map/ppermute | solution.py:22
  24.8 8.8 %collective-permute-start.10 = (bf16[2,32,1408]{2,1,0:T(8,128)(2,1)S(1)}, bf16[2,32,1408]{2,1,0:T(8,128)(2,1)S(1)}, u32[]{:S(2)}, u32[]{:S(2)}) collective-permute-start(bf16[2,32,1408]{2,1,0:T(8,128)(2,1)S(1)} %get-tuple-element.54), channel_id=1, source_target_pairs={{0,4},{4,8},{8,12},{12,0},{1,5},{5,9},{9,13},{13,1},{2,6},{6,10},{... | collective-permute-start | bytes 540680 | tf_op jit(solution)/shard_map/ppermute | solution.py:22
  26.4 10.0 %collective-permute-start.11 = (bf16[2,32,1408]{2,1,0:T(8,128)(2,1)S(1)}, bf16[2,32,1408]{2,1,0:T(8,128)(2,1)S(1)}, u32[]{:S(2)}, u32[]{:S(2)}) collective-permute-start(bf16[2,32,1408]{2,1,0:T(8,128)(2,1)S(1)} %get-tuple-element.54), channel_id=1, source_target_pairs={{0,12},{4,0},{8,4},{12,8},{1,13},{5,1},{9,5},{13,9},{2,14},{6,2},{... | collective-permute-start | bytes 540680 | tf_op jit(solution)/shard_map/ppermute | solution.py:22
  29.1 9.7 %collective-permute-start.12 = (bf16[2,32,1408]{2,1,0:T(8,128)(2,1)S(1)}, bf16[2,32,1408]{2,1,0:T(8,128)(2,1)S(1)}, u32[]{:S(2)}, u32[]{:S(2)}) collective-permute-start(bf16[2,32,1408]{2,1,0:T(8,128)(2,1)S(1)} %get-tuple-element.54), channel_id=1, source_target_pairs={{0,8},{4,12},{8,0},{12,4},{1,9},{5,13},{9,1},{13,5},{2,10},{6,14},... | collective-permute-start | bytes 540680 | tf_op jit(solution)/shard_map/ppermute | solution.py:22
  31.0 9.0 %collective-permute-start.1 = (bf16[128,1024]{1,0:T(8,128)(2,1)S(1)}, bf16[128,1024]{1,0:T(8,128)(2,1)S(1)}, u32[]{:S(2)}, u32[]{:S(2)}) collective-permute-start(bf16[128,1024]{1,0:T(8,128)(2,1)S(1)} %fusion.20), channel_id=1, source_target_pairs={{0,2},{2,0},{1,3},{3,1},{4,6},{6,4},{5,7},{7,5},{8,10},{10,8},{9,1... | collective-permute-start | bytes 786440 | tf_op jit(solution)/shard_map/ppermute | solution.py:26
  32.7 14.1 %collective-permute-start.6 = (bf16[2,4,32,768]{3,2,1,0:T(8,128)(2,1)S(1)}, bf16[2,4,32,768]{3,2,1,0:T(8,128)(2,1)S(1)}, u32[]{:S(2)}, u32[]{:S(2)}) collective-permute-start(bf16[2,4,32,768]{3,2,1,0:T(8,128)(2,1)S(1)} %bitcast_dynamic-update-slice_fusion.14), channel_id=1, source_target_pairs={{0,4},{4,8},{8,12},{12,0},{1,5},{5,9},{9,13},{13,1},{2,6},{6,10},{... | collective-permute-start | bytes 1179656 | tf_op jit(solution)/shard_map/ppermute | solution.py:22
  33.6 14.6 %collective-permute-start.7 = (bf16[2,4,32,768]{3,2,1,0:T(8,128)(2,1)S(1)}, bf16[2,4,32,768]{3,2,1,0:T(8,128)(2,1)S(1)}, u32[]{:S(2)}, u32[]{:S(2)}) collective-permute-start(bf16[2,4,32,768]{3,2,1,0:T(8,128)(2,1)S(1)} %bitcast_dynamic-update-slice_fusion.14), channel_id=1, source_target_pairs={{0,12},{4,0},{8,4},{12,8},{1,13},{5,1},{9,5},{13,9},{2,14},{6,2},{... | collective-permute-start | bytes 1179656 | tf_op jit(solution)/shard_map/ppermute | solution.py:22
  36.3 21.0 %collective-permute-start.8 = (bf16[2,4,32,768]{3,2,1,0:T(8,128)(2,1)S(1)}, bf16[2,4,32,768]{3,2,1,0:T(8,128)(2,1)S(1)}, u32[]{:S(2)}, u32[]{:S(2)}) collective-permute-start(bf16[2,4,32,768]{3,2,1,0:T(8,128)(2,1)S(1)} %bitcast_dynamic-update-slice_fusion.14), channel_id=1, source_target_pairs={{0,8},{4,12},{8,0},{12,4},{1,9},{5,13},{9,1},{13,5},{2,10},{6,14},... | collective-permute-start | bytes 1179656 | tf_op jit(solution)/shard_map/ppermute | solution.py:22
  38.8 27.3 %collective-permute-start.13 = (bf16[2,4,32,1408]{3,2,1,0:T(8,128)(2,1)S(1)}, bf16[2,4,32,1408]{3,2,1,0:T(8,128)(2,1)S(1)}, u32[]{:S(2)}, u32[]{:S(2)}) collective-permute-start(bf16[2,4,32,1408]{3,2,1,0:T(8,128)(2,1)S(1)} %bitcast_dynamic-update-slice_fusion.7), channel_id=1, source_target_pairs={{0,16},{16,32},{32,48},{48,0},{1,17},{17,33},{33,49},{49,1},{2,18}... | collective-permute-start | bytes 2162696 | tf_op jit(solution)/shard_map/ppermute | solution.py:22
  40.0 29.5 %collective-permute-start.14 = (bf16[2,4,32,1408]{3,2,1,0:T(8,128)(2,1)S(1)}, bf16[2,4,32,1408]{3,2,1,0:T(8,128)(2,1)S(1)}, u32[]{:S(2)}, u32[]{:S(2)}) collective-permute-start(bf16[2,4,32,1408]{3,2,1,0:T(8,128)(2,1)S(1)} %bitcast_dynamic-update-slice_fusion.7), channel_id=1, source_target_pairs={{0,48},{16,0},{32,16},{48,32},{1,49},{17,1},{33,17},{49,33},{2,50}... | collective-permute-start | bytes 2162696 | tf_op jit(solution)/shard_map/ppermute | solution.py:22
  46.8 10.6 %collective-permute-start.2 = (bf16[256,1024]{1,0:T(8,128)(2,1)S(1)}, bf16[256,1024]{1,0:T(8,128)(2,1)S(1)}, u32[]{:S(2)}, u32[]{:S(2)}) collective-permute-start(bf16[256,1024]{1,0:T(8,128)(2,1)S(1)} %pad_maximum_fusion.9), channel_id=1, source_target_pairs={{0,1},{1,0},{2,3},{3,2},{4,5},{5,4},{6,7},{7,6},{8,9},{9,8},{10,11... | collective-permute-start | bytes 1572872 | tf_op jit(solution)/shard_map/ppermute | solution.py:26
  66.1 14.8 %collective-permute-start.15 = (bf16[1,4,32,1408]{3,2,1,0:T(8,128)(2,1)S(1)}, bf16[1,4,32,1408]{3,2,1,0:T(8,128)(2,1)S(1)}, u32[]{:S(2)}, u32[]{:S(2)}) collective-permute-start(bf16[1,4,32,1408]{3,2,1,0:T(8,128)(2,1)S(1)} %slice.280), channel_id=1, source_target_pairs={{0,16},{16,32},{32,48},{48,0},{1,17},{17,33},{33,49},{49,1},{2,18}... | collective-permute-start | bytes 1081352 | tf_op jit(solution)/shard_map/ppermute | solution.py:22
  69.5 13.7 %collective-permute-start.16 = (bf16[1,4,32,1408]{3,2,1,0:T(8,128)(2,1)S(1)}, bf16[1,4,32,1408]{3,2,1,0:T(8,128)(2,1)S(1)}, u32[]{:S(2)}, u32[]{:S(2)}) collective-permute-start(bf16[1,4,32,1408]{3,2,1,0:T(8,128)(2,1)S(1)} %slice.281), channel_id=1, source_target_pairs={{0,48},{16,0},{32,16},{48,32},{1,49},{17,1},{33,17},{49,33},{2,50}... | collective-permute-start | bytes 1081352 | tf_op jit(solution)/shard_map/ppermute | solution.py:22
  86.2 9.2 %collective-permute-start.18 = (bf16[128,1024]{1,0:T(8,128)(2,1)S(1)}, bf16[128,1024]{1,0:T(8,128)(2,1)S(1)}, u32[]{:S(2)}, u32[]{:S(2)}) collective-permute-start(bf16[128,1024]{1,0:T(8,128)(2,1)S(1)} %slice.415), channel_id=1, source_target_pairs={{0,2},{2,0},{1,3},{3,1},{4,6},{6,4},{5,7},{7,5},{8,10},{10,8},{9,1... | collective-permute-start | bytes 786440 | tf_op jit(solution)/shard_map/ppermute | solution.py:26
  87.2 13.8 %collective-permute-start.21 = (bf16[128,1024]{0,1:T(8,128)(2,1)S(1)}, bf16[128,1024]{0,1:T(8,128)(2,1)S(1)}, u32[]{:S(2)}, u32[]{:S(2)}) collective-permute-start(bf16[128,1024]{0,1:T(8,128)(2,1)S(1)} %copy.34), channel_id=1, source_target_pairs={{0,2},{2,0},{1,3},{3,1},{4,6},{6,4},{5,7},{7,5},{8,10},{10,8},{9,1... | collective-permute-start | bytes 786440 | tf_op jit(solution)/shard_map/ppermute | solution.py:26
  95.8 10.3 %collective-permute-start.19 = (bf16[128,1024]{1,0:T(8,128)(2,1)S(1)}, bf16[128,1024]{1,0:T(8,128)(2,1)S(1)}, u32[]{:S(2)}, u32[]{:S(2)}) collective-permute-start(bf16[128,1024]{1,0:T(8,128)(2,1)S(1)} %multiply_convert_fusion.4), channel_id=1, source_target_pairs={{0,2},{2,0},{1,3},{3,1},{4,6},{6,4},{5,7},{7,5},{8,10},{10,8},{9,1... | collective-permute-start | bytes 786440 | tf_op jit(solution)/shard_map/ppermute | solution.py:26
  131.2 34.2 %all-to-all-start = ((bf16[4,256,1152]{2,1,0:T(8,128)(2,1)}), bf16[4,256,1152]{2,1,0:T(8,128)(2,1)S(1)}, u32[]{:S(2)}, u32[]{:S(2)}) async-start(bf16[4,256,1152]{2,1,0:T(8,128)(2,1)} %bitcast.207), calls=%async_computation | async-start | bytes 4718592 | tf_op jit(solution)/shard_map/all_to_all | solution.py:102
  137.2 8.5 %collective-permute-start.24 = (bf16[128,1024]{1,0:T(8,128)(2,1)S(1)}, bf16[128,1024]{1,0:T(8,128)(2,1)S(1)}, u32[]{:S(2)}, u32[]{:S(2)}) collective-permute-start(bf16[128,1024]{1,0:T(8,128)(2,1)S(1)} %slice.414), channel_id=1, source_target_pairs={{0,2},{2,0},{1,3},{3,1},{4,6},{6,4},{5,7},{7,5},{8,10},{10,8},{9,1... | collective-permute-start | bytes 786440 | tf_op jit(solution)/shard_map/ppermute | solution.py:26
  146.9 19.7 %collective-permute-start.25 = (bf16[128,1024]{1,0:T(8,128)(2,1)S(1)}, bf16[128,1024]{1,0:T(8,128)(2,1)}, u32[]{:S(2)}, u32[]{:S(2)}) collective-permute-start(bf16[128,1024]{1,0:T(8,128)(2,1)S(1)} %get-tuple-element.43), channel_id=1, source_target_pairs={{0,2},{2,0},{1,3},{3,1},{4,6},{6,4},{5,7},{7,5},{8,10},{10,8},{9,1... | collective-permute-start | bytes 786440 | tf_op jit(solution)/shard_map/ppermute | solution.py:26
  150.5 17.4 %collective-permute-start.27 = (bf16[256,1024]{1,0:T(8,128)(2,1)}, bf16[256,1024]{1,0:T(8,128)(2,1)}, u32[]{:S(2)}, u32[]{:S(2)}) collective-permute-start(bf16[256,1024]{1,0:T(8,128)(2,1)} %slice.409), channel_id=1, source_target_pairs={{0,1},{1,0},{2,3},{3,2},{4,5},{5,4},{6,7},{7,6},{8,9},{9,8},{10,11... | collective-permute-start | bytes 1572872 | tf_op jit(solution)/shard_map/ppermute | solution.py:26
  170.3 31.7 %collective-permute-start.28 = (bf16[128,1024]{1,0:T(8,128)(2,1)}, bf16[128,1024]{1,0:T(8,128)(2,1)}, u32[]{:S(2)}, u32[]{:S(2)}) collective-permute-start(bf16[128,1024]{1,0:T(8,128)(2,1)} %slice.413), channel_id=1, source_target_pairs={{0,2},{2,0},{1,3},{3,1},{4,6},{6,4},{5,7},{7,5},{8,10},{10,8},{9,1... | collective-permute-start | bytes 786440 | tf_op jit(solution)/shard_map/ppermute | solution.py:26
  189.7 49.4 %all-to-all-start.1 = ((bf16[32,32,1152]{2,1,0:T(8,128)(2,1)}), bf16[32,32,1152]{2,1,0:T(8,128)(2,1)S(1)}, u32[]{:S(2)}, u32[]{:S(2)}) async-start(bf16[32,32,1152]{2,1,0:T(8,128)(2,1)} %pad_maximum_fusion), calls=%async_computation.1 | async-start | bytes 4718592 | tf_op jit(solution)/shard_map/all_to_all | solution.py:102
  201.9 43.4 %reduce-scatter.5.cloned.1.call-start = ((), (), s32[]{:S(2)}) async-start(), calls=%async_computation.6 | async-start | bytes 1474560 | tf_op jit(solution)/shard_map/reduce_scatter | solution.py:230
  208.8 25.6 %collective-permute-start.34 = (bf16[2,32,1152]{2,1,0:T(8,128)(2,1)}, bf16[2,32,1152]{2,1,0:T(8,128)(2,1)S(1)}, u32[]{:S(2)}, u32[]{:S(2)}) collective-permute-start(bf16[2,32,1152]{2,1,0:T(8,128)(2,1)} %get-tuple-element.72), channel_id=1, source_target_pairs={{0,4},{4,8},{8,12},{12,0},{1,5},{5,9},{9,13},{13,1},{2,6},{6,10},{... | collective-permute-start | bytes 442376 | tf_op jit(solution)/shard_map/ppermute | solution.py:22
  210.6 23.8 %collective-permute-start.35 = (bf16[2,32,1152]{2,1,0:T(8,128)(2,1)}, bf16[2,32,1152]{2,1,0:T(8,128)(2,1)S(1)}, u32[]{:S(2)}, u32[]{:S(2)}) collective-permute-start(bf16[2,32,1152]{2,1,0:T(8,128)(2,1)} %get-tuple-element.73), channel_id=1, source_target_pairs={{0,12},{4,0},{8,4},{12,8},{1,13},{5,1},{9,5},{13,9},{2,14},{6,2},{... | collective-permute-start | bytes 442376 | tf_op jit(solution)/shard_map/ppermute | solution.py:22
  213.9 22.9 %collective-permute-start.36 = (bf16[2,32,1152]{2,1,0:T(8,128)(2,1)S(1)}, bf16[2,32,1152]{2,1,0:T(8,128)(2,1)S(1)}, u32[]{:S(2)}, u32[]{:S(2)}) collective-permute-start(bf16[2,32,1152]{2,1,0:T(8,128)(2,1)S(1)} %fusion.52), channel_id=1, source_target_pairs={{0,8},{4,12},{8,0},{12,4},{1,9},{5,13},{9,1},{13,5},{2,10},{6,14},... | collective-permute-start | bytes 442376 | tf_op jit(solution)/shard_map/ppermute | solution.py:22
  217.5 20.3 %collective-permute-start.31 = (bf16[128,1024]{1,0:T(8,128)(2,1)S(1)}, bf16[128,1024]{1,0:T(8,128)(2,1)S(1)}, u32[]{:S(2)}, u32[]{:S(2)}) collective-permute-start(bf16[128,1024]{1,0:T(8,128)(2,1)S(1)} %slice.412), channel_id=1, source_target_pairs={{0,2},{2,0},{1,3},{3,1},{4,6},{6,4},{5,7},{7,5},{8,10},{10,8},{9,1... | collective-permute-start | bytes 786440 | tf_op jit(solution)/shard_map/ppermute | solution.py:26
  247.6 8.9 %collective-permute-start.37 = (bf16[32,3456]{1,0:T(8,128)(2,1)S(1)}, bf16[32,3456]{1,0:T(8,128)(2,1)S(1)}, u32[]{:S(2)}, u32[]{:S(2)}) collective-permute-start(bf16[32,3456]{1,0:T(8,128)(2,1)S(1)} %fusion.47), channel_id=1, source_target_pairs={{0,64},{64,0},{1,65},{65,1},{2,66},{66,2},{3,67},{67,3},{4,68},{68... | collective-permute-start | bytes 663560 | tf_op jit(solution)/shard_map/ppermute | solution.py:26
  (50 other events, 231.1 us)
Sparse Core Ops, SparseCore 0:
  14.5 85.0 all-gather.1
  129.2 53.3 reduce-scatter.2
  213.1 32.2 reduce-scatter.4
